TPU v7x, 32 devices: a whole 2x2x4 slice. The times are simulated.
32 devices in a mesh: dp: 4 (over x, core), fsdp: 8 (over z, y).
Axes of the slice: x: 2, y: 2, z: 4, core: 2. Of those that a mesh axis runs over, the one named last changes fastest.
Arguments:
- text_in: bfloat16 [512, 64, 768], P(('dp', 'fsdp')), may hold values from -6 to 6
- text_segments: int32 [512, 64], P(('dp', 'fsdp')), may hold values from 0 to 8, never falling along the last dimension, each value on 1 to 32 neighbouring positions
- text_cotangent: bfloat16 [512, 64, 768], P(('dp', 'fsdp')), may hold values from -6 to 6
- image_in: bfloat16 [128, 50, 768], P(('dp', 'fsdp')), may hold values from -6 to 6
- ln1_gain: bfloat16 [768], P('fsdp'), may hold values from 0.25 to 1.75
- ln1_bias: bfloat16 [768], P('fsdp'), may hold values from -4 to 4
- w_qkv: bfloat16 [768, 2304], P('fsdp'), may hold values from -0.21875 to 0.21875
- q_bias: bfloat16 [768], P('fsdp'), may hold values from -4 to 4
- v_bias: bfloat16 [768], P('fsdp'), may hold values from -4 to 4
- w_out: bfloat16 [768, 768], P('fsdp'), may hold values from -0.625 to 0.625
- out_bias: bfloat16 [768], P('fsdp'), may hold values from -4 to 4
- ln2_gain: bfloat16 [768], P('fsdp'), may hold values from 0.25 to 1.75
- ln2_bias: bfloat16 [768], P('fsdp'), may hold values from -4 to 4
- w_fc1: bfloat16 [768, 3072], P('fsdp'), may hold values from -0.21875 to 0.21875
- fc1_bias: bfloat16 [3072], P('fsdp'), may hold values from -4 to 4
- w_fc2: bfloat16 [3072, 768], P('fsdp'), may hold values from -0.109375 to 0.109375
- fc2_bias: bfloat16 [768], P('fsdp'), may hold values from -4 to 4
- image_norms: bfloat16 [2, 768], P(None, 'fsdp'), may hold values from 0.25 to 1.75
- image_qkv: bfloat16 [768, 2304], P('fsdp'), may hold values from -0.21875 to 0.21875
- image_proj: bfloat16 [768, 768], P('fsdp'), may hold values from -0.625 to 0.625
- image_fc1: bfloat16 [768, 3072], P('fsdp'), may hold values from -0.21875 to 0.21875
- image_fc2: bfloat16 [3072, 768], P('fsdp'), may hold values from -0.109375 to 0.109375
Outputs:
- text_out: bfloat16 [512, 64, 768], P(('dp', 'fsdp'))
- image_out: bfloat16 [128, 50, 768], P(('dp', 'fsdp'))
- text_grad: float32 [512, 64, 768], P(('dp', 'fsdp'))
- grad_ln1_gain: float32 [768], P('fsdp')
- grad_ln1_bias: float32 [768], P('fsdp')
- grad_qkv: float32 [768, 2304], P('fsdp')
- grad_q_bias: float32 [768], P('fsdp')
- grad_v_bias: float32 [768], P('fsdp')
- grad_w_out: float32 [768, 768], P('fsdp')
- grad_out_bias: float32 [768], P('fsdp')
- grad_ln2_gain: float32 [768], P('fsdp')
- grad_ln2_bias: float32 [768], P('fsdp')
- grad_fc1: float32 [768, 3072], P('fsdp')
- grad_fc1_bias: float32 [3072], P('fsdp')
- grad_fc2: float32 [3072, 768], P('fsdp')
- grad_fc2_bias: float32 [768], P('fsdp')
Inputs may be any that keep to these rules, and one draw needn't show every extreme that they name: `text_segments`: along each row ids never fall; each id covers 1 to 32 positions and every id from 0 to 8 appears in every row.
All inputs are finite; a program needn't handle non-finite values.
Results may differ from a plain program's by a relative error of at most 0.015.
Values may be sent and summed in bfloat16 or wider, within the bound.
No kernel may reach another device: no remote copies, remote signals or barrier semaphores. Data moves between devices by JAX's collectives and lax.ppermute only.
A program may use at most 256 MiB of HBM per device.

v0:
```python
from functools import partial

import jax
import jax.numpy as jnp
from jax import lax
from jax.sharding import PartitionSpec as P

HEADS = 12


epsilon = 1e-06


def normed(values, scale_by, shift_by):
    centre = values - jnp.mean(values, axis=-1, keepdims=True)
    spread = lax.rsqrt(jnp.mean(centre * centre, axis=-1, keepdims=True) + epsilon)
    return centre * spread * scale_by + shift_by


def norm_pullback(values, scale_by, shift_by, grad_result):
    result, pullback = jax.vjp(normed, values, scale_by, shift_by)
    return pullback(grad_result)


def forward_block(
    inputs, allowed, norms, w_qkv, qkv_bias, w_out, out_bias, w_fc1, fc1_bias, w_fc2, fc2_bias
):
    batch_rows, length, model_width = inputs.shape
    head_dim = model_width // HEADS
    inflow = inputs.reshape(batch_rows * length, model_width).astype(jnp.float32)
    norm_one = normed(inflow, norms[0], norms[1]).astype(jnp.bfloat16)
    joined = (jnp.dot(norm_one, w_qkv, preferred_element_type=jnp.float32) + qkv_bias).astype(
        jnp.bfloat16
    )
    parted = joined.reshape(batch_rows, length, 3, HEADS, head_dim)
    queries, key_heads, value_heads = (parted[:, :, 0], parted[:, :, 1], parted[:, :, 2])
    scores = jnp.einsum(
        "rqhe,rkhe->rhqk", queries, key_heads, preferred_element_type=jnp.float32
    ) * head_dim ** (-0.5)
    if allowed is not None:
        scores = jnp.where(allowed[:, None], scores, -1e30)
    largest = jnp.max(scores, axis=-1, keepdims=True)
    raised = jnp.exp(scores - largest)
    totals = jnp.sum(raised, axis=-1, keepdims=True)
    attend = (raised / totals).astype(jnp.bfloat16)
    mixed_heads = jnp.einsum(
        "rhqk,rkhe->rqhe", attend, value_heads, preferred_element_type=jnp.float32
    )
    mixed_heads = mixed_heads.reshape(batch_rows * length, model_width).astype(jnp.bfloat16)
    hidden = inflow + jnp.dot(mixed_heads, w_out, preferred_element_type=jnp.float32) + out_bias
    norm_two = normed(hidden, norms[2], norms[3]).astype(jnp.bfloat16)
    pre_act = jnp.dot(norm_two, w_fc1, preferred_element_type=jnp.float32) + fc1_bias
    active = jax.nn.gelu(pre_act, approximate=False).astype(jnp.bfloat16)
    output = hidden + jnp.dot(active, w_fc2, preferred_element_type=jnp.float32) + fc2_bias
    stored = (
        inflow,
        norm_one,
        queries,
        key_heads,
        value_heads,
        largest + jnp.log(totals),
        mixed_heads,
        hidden,
        norm_two,
        pre_act,
        active,
    )
    return (output.reshape(batch_rows, length, model_width).astype(jnp.bfloat16), stored)


def per_device(
    text_in,
    text_segments,
    text_cotangent,
    image_in,
    ln1_gain,
    ln1_bias,
    w_qkv,
    q_bias,
    v_bias,
    w_out,
    out_bias,
    ln2_gain,
    ln2_bias,
    w_fc1,
    fc1_bias,
    w_fc2,
    fc2_bias,
    image_norms,
    image_qkv,
    image_proj,
    image_fc1,
    image_fc2,
):
    whole = (
        lax.all_gather(ln1_gain, "fsdp", axis=0, tiled=True),
        lax.all_gather(ln1_bias, "fsdp", axis=0, tiled=True),
        lax.all_gather(w_qkv, "fsdp", axis=0, tiled=True),
        lax.all_gather(q_bias, "fsdp", axis=0, tiled=True),
        lax.all_gather(v_bias, "fsdp", axis=0, tiled=True),
        lax.all_gather(w_out, "fsdp", axis=0, tiled=True),
        lax.all_gather(out_bias, "fsdp", axis=0, tiled=True),
        lax.all_gather(ln2_gain, "fsdp", axis=0, tiled=True),
        lax.all_gather(ln2_bias, "fsdp", axis=0, tiled=True),
        lax.all_gather(w_fc1, "fsdp", axis=0, tiled=True),
        lax.all_gather(fc1_bias, "fsdp", axis=0, tiled=True),
        lax.all_gather(w_fc2, "fsdp", axis=0, tiled=True),
        lax.all_gather(fc2_bias, "fsdp", axis=0, tiled=True),
    )
    image_whole = (
        lax.all_gather(image_norms, "fsdp", axis=1, tiled=True),
        lax.all_gather(image_qkv, "fsdp", axis=0, tiled=True),
        lax.all_gather(image_proj, "fsdp", axis=0, tiled=True),
        lax.all_gather(image_fc1, "fsdp", axis=0, tiled=True),
        lax.all_gather(image_fc2, "fsdp", axis=0, tiled=True),
    )
    image_gains = image_whole[0].astype(jnp.float32)
    image_norm_set = (image_gains[0], 0.0, image_gains[1], 0.0)
    image_out, image_stored = forward_block(
        image_in,
        None,
        image_norm_set,
        image_whole[1],
        0.0,
        image_whole[2],
        0.0,
        image_whole[3],
        0.0,
        image_whole[4],
        0.0,
    )
    vectors = [item.astype(jnp.float32) for item in whole]
    gain_one, bias_one, gain_two, bias_two = (vectors[0], vectors[1], vectors[7], vectors[8])
    model_width = whole[0].shape[0]
    qkv_bias = jnp.concatenate([vectors[3], jnp.zeros_like(vectors[3]), vectors[4]])
    allowed = text_segments[:, :, None] == text_segments[:, None, :]
    text_out, stored = forward_block(
        text_in,
        allowed,
        (gain_one, bias_one, gain_two, bias_two),
        whole[2],
        qkv_bias,
        whole[5],
        vectors[6],
        whole[9],
        vectors[10],
        whole[11],
        vectors[12],
    )
    (
        inflow,
        norm_one,
        queries,
        key_heads,
        value_heads,
        log_total,
        mixed_heads,
        hidden,
        norm_two,
        pre_act,
        active,
    ) = stored
    back_qkv, back_out, back_fc1, back_fc2 = (
        lax.all_gather(w_qkv, "fsdp", axis=0, tiled=True),
        lax.all_gather(w_out, "fsdp", axis=0, tiled=True),
        lax.all_gather(w_fc1, "fsdp", axis=0, tiled=True),
        lax.all_gather(w_fc2, "fsdp", axis=0, tiled=True),
    )
    batch_rows, length = text_segments.shape
    head_dim = model_width // HEADS
    scale_factor = head_dim ** (-0.5)
    grad_flow = text_cotangent.reshape(batch_rows * length, model_width).astype(jnp.float32)
    branch_two = grad_flow.astype(jnp.bfloat16)
    grad_fc2 = jnp.einsum("nf,nd->fd", active, branch_two, preferred_element_type=jnp.float32)
    grad_fc2_bias = jnp.sum(branch_two.astype(jnp.float32), axis=0)
    grad_active = jnp.einsum("nd,fd->nf", branch_two, back_fc2, preferred_element_type=jnp.float32)
    gelu_value, gelu_back = jax.vjp(partial(jax.nn.gelu, approximate=False), pre_act)
    grad_pre = gelu_back(grad_active)[0].astype(jnp.bfloat16)
    grad_fc1 = jnp.einsum("nd,nf->df", norm_two, grad_pre, preferred_element_type=jnp.float32)
    grad_fc1_bias = jnp.sum(grad_pre.astype(jnp.float32), axis=0)
    grad_norm_two = jnp.einsum("nf,df->nd", grad_pre, back_fc1, preferred_element_type=jnp.float32)
    hidden_part, grad_ln2_gain, grad_ln2_bias = norm_pullback(
        hidden, gain_two, bias_two, grad_norm_two
    )
    grad_hidden = grad_flow + hidden_part
    branch_one = grad_hidden.astype(jnp.bfloat16)
    grad_w_out = jnp.einsum(
        "ne,nd->ed", mixed_heads, branch_one, preferred_element_type=jnp.float32
    )
    grad_out_bias = jnp.sum(branch_one.astype(jnp.float32), axis=0)
    grad_mixed = jnp.einsum(
        "nd,ed->ne", branch_one, back_out, preferred_element_type=jnp.float32
    ).astype(jnp.bfloat16)
    grad_mixed = grad_mixed.reshape(batch_rows, length, HEADS, head_dim)
    scores = (
        jnp.einsum("rqhe,rkhe->rhqk", queries, key_heads, preferred_element_type=jnp.float32)
        * scale_factor
    )
    attend = jnp.where(allowed[:, None], jnp.exp(scores - log_total), 0.0)
    attend_low = attend.astype(jnp.bfloat16)
    grad_values = jnp.einsum(
        "rhqk,rqhe->rkhe", attend_low, grad_mixed, preferred_element_type=jnp.float32
    )
    grad_attend = jnp.einsum(
        "rqhe,rkhe->rhqk", grad_mixed, value_heads, preferred_element_type=jnp.float32
    )
    centred = grad_attend - jnp.sum(grad_attend * attend, axis=-1, keepdims=True)
    grad_scores = (attend * centred).astype(jnp.bfloat16)
    grad_queries = (
        jnp.einsum("rhqk,rkhe->rqhe", grad_scores, key_heads, preferred_element_type=jnp.float32)
        * scale_factor
    )
    grad_keys = (
        jnp.einsum("rhqk,rqhe->rkhe", grad_scores, queries, preferred_element_type=jnp.float32)
        * scale_factor
    )
    grad_joined = jnp.stack([grad_queries, grad_keys, grad_values], axis=2)
    grad_joined = grad_joined.reshape(batch_rows * length, 3 * model_width).astype(jnp.bfloat16)
    grad_qkv = jnp.einsum("nd,nf->df", norm_one, grad_joined, preferred_element_type=jnp.float32)
    column_sums = jnp.sum(grad_joined.astype(jnp.float32), axis=0)
    grad_q_bias = column_sums[:model_width]
    grad_v_bias = column_sums[2 * model_width :]
    grad_norm_one = jnp.einsum(
        "nf,df->nd", grad_joined, back_qkv, preferred_element_type=jnp.float32
    )
    inflow_part, grad_ln1_gain, grad_ln1_bias = norm_pullback(
        inflow, gain_one, bias_one, grad_norm_one
    )
    text_grad = (grad_hidden + inflow_part).reshape(batch_rows, length, model_width)
    shares = (
        lax.psum_scatter(grad_ln1_gain, "fsdp", scatter_dimension=0, tiled=True),
        lax.psum_scatter(grad_ln1_bias, "fsdp", scatter_dimension=0, tiled=True),
        lax.psum_scatter(grad_qkv, "fsdp", scatter_dimension=0, tiled=True),
        lax.psum_scatter(grad_q_bias, "fsdp", scatter_dimension=0, tiled=True),
        lax.psum_scatter(grad_v_bias, "fsdp", scatter_dimension=0, tiled=True),
        lax.psum_scatter(grad_w_out, "fsdp", scatter_dimension=0, tiled=True),
        lax.psum_scatter(grad_out_bias, "fsdp", scatter_dimension=0, tiled=True),
        lax.psum_scatter(grad_ln2_gain, "fsdp", scatter_dimension=0, tiled=True),
        lax.psum_scatter(grad_ln2_bias, "fsdp", scatter_dimension=0, tiled=True),
        lax.psum_scatter(grad_fc1, "fsdp", scatter_dimension=0, tiled=True),
        lax.psum_scatter(grad_fc1_bias, "fsdp", scatter_dimension=0, tiled=True),
        lax.psum_scatter(grad_fc2, "fsdp", scatter_dimension=0, tiled=True),
        lax.psum_scatter(grad_fc2_bias, "fsdp", scatter_dimension=0, tiled=True),
    )
    summed = (
        lax.psum(shares[0].astype(jnp.bfloat16), "dp").astype(jnp.float32),
        lax.psum(shares[1].astype(jnp.bfloat16), "dp").astype(jnp.float32),
        lax.psum(shares[2].astype(jnp.bfloat16), "dp").astype(jnp.float32),
        lax.psum(shares[3].astype(jnp.bfloat16), "dp").astype(jnp.float32),
        lax.psum(shares[4].astype(jnp.bfloat16), "dp").astype(jnp.float32),
        lax.psum(shares[5].astype(jnp.bfloat16), "dp").astype(jnp.float32),
        lax.psum(shares[6].astype(jnp.bfloat16), "dp").astype(jnp.float32),
        lax.psum(shares[7].astype(jnp.bfloat16), "dp").astype(jnp.float32),
        lax.psum(shares[8].astype(jnp.bfloat16), "dp").astype(jnp.float32),
        lax.psum(shares[9].astype(jnp.bfloat16), "dp").astype(jnp.float32),
        lax.psum(shares[10].astype(jnp.bfloat16), "dp").astype(jnp.float32),
        lax.psum(shares[11].astype(jnp.bfloat16), "dp").astype(jnp.float32),
        lax.psum(shares[12].astype(jnp.bfloat16), "dp").astype(jnp.float32),
    )
    return (
        text_out,
        image_out,
        text_grad,
        summed[0],
        summed[1],
        summed[2],
        summed[3],
        summed[4],
        summed[5],
        summed[6],
        summed[7],
        summed[8],
        summed[9],
        summed[10],
        summed[11],
        summed[12],
    )


def solution(mesh):
    in_specs = (
        P(("dp", "fsdp"), None, None),
        P(("dp", "fsdp"), None),
        P(("dp", "fsdp"), None, None),
        P(("dp", "fsdp"), None, None),
        P("fsdp"),
        P("fsdp"),
        P("fsdp", None),
        P("fsdp"),
        P("fsdp"),
        P("fsdp", None),
        P("fsdp"),
        P("fsdp"),
        P("fsdp"),
        P("fsdp", None),
        P("fsdp"),
        P("fsdp", None),
        P("fsdp"),
        P(None, "fsdp"),
        P("fsdp", None),
        P("fsdp", None),
        P("fsdp", None),
        P("fsdp", None),
    )
    out_specs = (
        P(("dp", "fsdp"), None, None),
        P(("dp", "fsdp"), None, None),
        P(("dp", "fsdp"), None, None),
        P("fsdp"),
        P("fsdp"),
        P("fsdp", None),
        P("fsdp"),
        P("fsdp"),
        P("fsdp", None),
        P("fsdp"),
        P("fsdp"),
        P("fsdp"),
        P("fsdp", None),
        P("fsdp"),
        P("fsdp", None),
        P("fsdp"),
    )
    return jax.shard_map(
        per_device, mesh=mesh, in_specs=in_specs, out_specs=out_specs, check_vma=False
    )
```

profile of v0, /device:TPU:11, one launch (start us, length us, event | category | flops | bytes accessed | tf_op | source)
XLA Modules:
  0.0 1149.4 jit_solution(9356741888228474004)
XLA Ops:
  16.9 27.7 %all-reduce.18 = (bf16[768]{0:T(1024)(128)(2,1)S(1)}, bf16[768]{0:T(1024)(128)(2,1)S(1)}, bf16[768]{0:T(1024)(128)(2,1)S(1)}, bf16[768]{0:T(1024)(128)(2,1)S(1)}...) all-reduce(bf16[768]{0:T(1024)(128)(2,1)S(1)} %dynamic-update-slice, ...), channel_id=1, replica_groups=mesh['dp'=4,'fsdp'=8] {'fsdp'}, use_global_device_ids=true, to_apply=%add.1 | all-reduce | flops 6144 | bytes 24576
  45.3 24.7 %all-gather = bf16[8,1,384]{2,1,0:T(2,128)(2,1)S(1)} all-gather(bf16[1,1,384]{2,1,0:T(2,128)(2,1)S(1)} %reshape.270), channel_id=1, replica_groups=mesh['dp'=4,'fsdp'=8] {'fsdp'}, dimensions={0}, use_global_device_ids=true | all-gather | bytes 6912 | tf_op jit(solution)/shard_map/all_gather | solution.py:106
  89.9 13.2 %reshape.239 = bf16[16,64,3,12,64]{1,0,4,3,2:T(8,128)(2,1)} reshape(bf16[1024,2304]{0,1:T(8,128)(2,1)} %copy.95) | data formatting | bytes 9437184 | tf_op jit(solution)/shard_map/reshape | solution.py:35
  128.8 15.2 %convert_bitcast_fusion = bf16[16,64,12,64]{1,3,2,0:T(8,128)(2,1)S(1)} fusion(f32[16,12,64,64]{2,3,1,0:T(8,128)S(1)} %get-tuple-element.140, f32[16,12,64]{2,1,0:T(8,128)S(1)} %fusion.7, f32[16,12,64]{2,1,0:T(8,128)S(1)} %get-tuple-element.139, pred[16,64,64]{1,2,0:T(8,128)(4,1)S(1)} %broadcast_compare_fusion, bf16[16,64,1,12,64]{1,0,4,3,2:T(8,128)(2,1)S(1)} %copy-done.12), kind=kOutput, calls=%fused_computation.76 | convolution fusion | flops 105381888 | bytes 6455296 | tf_op jit(solution)/shard_map/rhqk,rkhe->rqhe/dot_general | solution.py:46
  158.4 39.6 %all-gather.15.cloned.1.call-done = bf16[768,3072]{1,0:T(8,128)(2,1)} async-done(((bf16[96,3072]{1,0:T(8,128)(2,1)}), bf16[768,3072]{1,0:T(8,128)(2,1)}) %all-gather.15.cloned.1.call-update) | async-done | bytes 4718608 | tf_op jit(solution)/shard_map/all_gather | solution.py:105
  198.0 37.9 %multiply_convert_fusion = (bf16[1024,3072]{1,0:T(8,128)(2,1)}, f32[1024,3072]{1,0:T(8,128)}, f32[1024,3072]{1,0:T(8,128)}) fusion(f32[3072]{0:T(1024)S(1)} %bitcast.151, bf16[768,3072]{1,0:T(8,128)(2,1)} %all-gather.15.cloned.1.call-done, f32[1024,768]{1,0:T(8,128)} %copy-done.3, f32[768]{0:T(1024)S(1)} %convert_element_type.256, ...), kind=kOutput, calls=%fused_computation.7 | convolution fusion | flops 5043388416 | bytes 39348224 | tf_op jit(solution)/shard_map/dot_general | solution.py:52
  235.9 42.2 %all-gather.17.cloned.1.call-done = bf16[3072,768]{1,0:T(8,128)(2,1)} async-done(((bf16[384,768]{1,0:T(8,128)(2,1)}), bf16[3072,768]{1,0:T(8,128)(2,1)}) %all-gather.17.cloned.1.call-update) | async-done | bytes 4718608 | tf_op jit(solution)/shard_map/all_gather | solution.py:107
  278.1 18.2 %convert_reduce_fusion.1 = (f32[3072]{0:T(1024)S(1)}, bf16[1024,3072]{1,0:T(8,128)(2,1)}) fusion(f32[1024,3072]{1,0:T(8,128)} %get-tuple-element.126, bf16[1024,768]{1,0:T(8,128)(2,1)} %bitcast.146, bf16[3072,768]{1,0:T(8,128)(2,1)} %all-gather.17.cloned.1.call-done, f32[1024,3072]{1,0:T(8,128)} %get-tuple-element.143, f32[3072]{0:T(1024)S(1)} %bitcast.152), kind=kOutput, calls=%fused_computation.5 | convolution fusion | flops 4885312512 | bytes 37773312 | tf_op jit(solution)/shard_map/nd,fd->nf/dot_general | solution.py:176
  296.3 9.6 multiply_reduce_fusion.1
  323.5 8.3 multiply_reduce_fusion
  353.5 13.5 %copy.116 = bf16[16,64,3,12,64]{1,0,4,3,2:T(8,128)(2,1)} copy(bf16[16,64,3,12,64]{4,1,3,0,2:T(8,128)(2,1)} %get-tuple-element.122) | data formatting | bytes 9437184 | tf_op jit(solution)/shard_map/convert_element_type | solution.py:218
  367.0 13.3 %convert_element_type.284 = bf16[1024,2304]{0,1:T(8,128)(2,1)} reshape(bf16[16,64,3,12,64]{1,0,4,3,2:T(8,128)(2,1)} %copy.116) | data formatting | bytes 9437184 | tf_op jit(solution)/shard_map/convert_element_type | solution.py:218
  380.4 9.6 fusion.135
  390.1 10.9 fusion.122
  402.4 10.2 fusion.137
  417.1 14.0 %all-gather.1 = bf16[8,96,2]{1,2,0:T(2,128)(2,1)S(1)} all-gather(bf16[1,96,2]{1,2,0:T(2,128)(2,1)S(1)} %bitcast.153), channel_id=1, replica_groups=mesh['dp'=4,'fsdp'=8] {'fsdp'}, dimensions={0}, use_global_device_ids=true | all-gather | bytes 3456 | tf_op jit(solution)/shard_map/all_gather | solution.py:111
  473.9 72.3 %all-gather.25.cloned.1.call-done = bf16[3072,768]{1,0:T(8,128)(2,1)} async-done(((bf16[384,768]{1,0:T(8,128)(2,1)}), bf16[3072,768]{1,0:T(8,128)(2,1)}) %all-gather.25.cloned.1.call-update) | async-done | bytes 4718608 | tf_op jit(solution)/shard_map/all_gather | solution.py:115
  546.2 11.6 %fusion.69 = bf16[200,768]{1,0:T(8,128)(2,1)} fusion(f32[200,768]{1,0:T(8,128)} %copy-done.17, bf16[3072,768]{1,0:T(8,128)(2,1)} %all-gather.25.cloned.1.call-done, bf16[768,3072]{1,0:T(8,128)(2,1)} %all-gather.23.cloned.1.call-done, f32[768]{0:T(1024)S(1)} %get-tuple-element.87, f32[200]{0:T(256)S(1)} %add_rsqrt_fusion.1, f32[200]{0:T(256)S(1)} %broadcast_multiply_fusion.3), kind=kOutput, calls=%fused_computation.114 | convolution fusion | flops 1928294400 | bytes 10363456 | tf_op jit(solution)/shard_map/dot_general | solution.py:54
  557.8 59.2 %reduce-scatter.7.cloned.1.call-done = f32[96,768]{1,0:T(8,128)} async-done(((f32[768,768]{1,0:T(8,128)}), f32[96,768]{1,0:T(8,128)}) %reduce-scatter.7.cloned.1.call-update) | async-done | bytes 294928 | tf_op jit(solution)/shard_map/reduce_scatter | solution.py:236
  618.6 130.8 %reduce-scatter.5.cloned.1.call-done = f32[96,2304]{1,0:T(8,128)} async-done(((f32[768,2304]{1,0:T(8,128)}), f32[96,2304]{1,0:T(8,128)}) %reduce-scatter.5.cloned.1.call-update) | async-done | bytes 884752 | tf_op jit(solution)/shard_map/reduce_scatter | solution.py:233
  751.3 164.2 %reduce-scatter.9.cloned.1.call-done = f32[96,3072]{1,0:T(8,128)} async-done(((f32[768,3072]{1,0:T(8,128)}), f32[96,3072]{1,0:T(8,128)}) %reduce-scatter.9.cloned.1.call-update) | async-done | bytes 1179664 | tf_op jit(solution)/shard_map/reduce_scatter | solution.py:240
  917.7 164.3 %reduce-scatter.11.cloned.1.call-done = f32[384,768]{1,0:T(8,128)} async-done(((f32[3072,768]{1,0:T(8,128)}), f32[384,768]{1,0:T(8,128)}) %reduce-scatter.11.cloned.1.call-update) | async-done | bytes 1179664 | tf_op jit(solution)/shard_map/reduce_scatter | solution.py:242
  1084.4 27.7 %all-reduce.17 = (bf16[768]{0:T(1024)(128)(2,1)S(1)}, bf16[768]{0:T(1024)(128)(2,1)S(1)}, bf16[768]{0:T(1024)(128)(2,1)S(1)}, bf16[768]{0:T(1024)(128)(2,1)S(1)}...) all-reduce(f32[768]{0:T(1024)S(1)} %get-tuple-element.82, ...), channel_id=2, replica_groups=mesh['dp'=4,'fsdp'=8] {'fsdp'}, use_global_device_ids=true, to_apply=%region_18.19.clone | all-reduce | flops 9216 | bytes 55296
  1112.8 12.5 %all-reduce.19 = (bf16[96]{0:T(256)(128)(2,1)S(1)}, bf16[96]{0:T(256)(128)(2,1)S(1)}, bf16[96]{0:T(256)(128)(2,1)S(1)}, bf16[96]{0:T(256)(128)(2,1)S(1)}, bf16[9...) all-reduce(bf16[96]{0:T(256)(128)(2,1)S(1)} %dynamic-slice.43, ...), channel_id=1, replica_groups=mesh['dp'=4,'fsdp'=8] {'dp'}, use_global_device_ids=true, to_apply=%region_19.20 | all-reduce | flops 1152 | bytes 4608 | tf_op jit(solution)/shard_map/psum | solution.py:246
  (265 shorter events, 181.6 us)
Async XLA Ops:
  7.2 68.6 %all-gather.11.cloned.1.call-start = ((), (), s32[]{:S(2)}) async-start(), calls=%async_computation.4 | async-start | bytes 3981312 | tf_op jit(solution)/shard_map/all_gather | solution.py:98
  8.0 144.7 %all-gather.13.cloned.1.call-start = ((), (), s32[]{:S(2)}) async-start(), calls=%async_computation.5 | async-start | bytes 1327104 | tf_op jit(solution)/shard_map/all_gather | solution.py:101
  8.8 35.9 %copy-start.31 = (s32[16,64]{1,0:T(8,128)S(1)}, s32[16,64]{1,0:T(8,128)}, u32[]{:S(2)}) copy-start(s32[16,64]{1,0:T(8,128)} %param.23) | copy-start | bytes 12292
  8.8 36.5 %copy-start.34 = (bf16[384]{0:T(512)(128)(2,1)S(1)}, bf16[384]{0:T(512)(128)(2,1)}, u32[]{:S(2)}) copy-start(bf16[384]{0:T(512)(128)(2,1)} %param.36) | copy-start | bytes 2308
  8.8 189.2 %all-gather.15.cloned.1.call-start = ((), (), s32[]{:S(2)}) async-start(), calls=%async_computation.6 | async-start | bytes 5308416 | tf_op jit(solution)/shard_map/all_gather | solution.py:105
  9.5 268.5 %all-gather.17.cloned.1.call-start = ((), (), s32[]{:S(2)}) async-start(), calls=%async_computation.7 | async-start | bytes 5308416 | tf_op jit(solution)/shard_map/all_gather | solution.py:107
  10.1 421.4 %all-gather.19.cloned.1.call-start = ((), (), s32[]{:S(2)}) async-start(), calls=%async_computation.8 | async-start | bytes 3981312 | tf_op jit(solution)/shard_map/all_gather | solution.py:112
  10.7 442.8 %all-gather.21.cloned.1.call-start = ((), (), s32[]{:S(2)}) async-start(), calls=%async_computation.9 | async-start | bytes 1327104 | tf_op jit(solution)/shard_map/all_gather | solution.py:113
  11.3 462.6 %all-gather.23.cloned.1.call-start = ((), (), s32[]{:S(2)}) async-start(), calls=%async_computation.10 | async-start | bytes 5308416 | tf_op jit(solution)/shard_map/all_gather | solution.py:114
  12.0 534.2 %all-gather.25.cloned.1.call-start = ((), (), s32[]{:S(2)}) async-start(), calls=%async_computation.11 | async-start | bytes 5308416 | tf_op jit(solution)/shard_map/all_gather | solution.py:115
  12.8 604.2 %reduce-scatter.7.cloned.1.call-start = ((), (), s32[]{:S(2)}) async-start(), calls=%async_computation.13 | async-start | bytes 2654208 | tf_op jit(solution)/shard_map/reduce_scatter | solution.py:236
  13.8 58.7 %copy-start.25 = (f32[1024]{0:T(1024)}, f32[1024]{0:T(1024)S(1)}, u32[]{:S(2)}) copy-start(f32[1024]{0:T(1024)S(1)} %div.73) | copy-start | bytes 12292
  44.6 27.8 %copy-start.23 = (f32[768]{0:T(1024)}, f32[768]{0:T(1024)S(1)}, u32[]{:S(2)}) copy-start(f32[768]{0:T(1024)S(1)} %convert_element_type.244) | copy-start | bytes 9220
  44.7 27.8 %copy-start.27 = (f32[1024]{0:T(1024)}, f32[1024]{0:T(1024)S(1)}, u32[]{:S(2)}) copy-start(f32[1024]{0:T(1024)S(1)} %rsqrt.44) | copy-start | bytes 12292
  278.1 18.2 %copy-start.4 = (f32[1024,768]{1,0:T(8,128)S(1)}, f32[1024,768]{1,0:T(8,128)}, u32[]{:S(2)}) copy-start(f32[1024,768]{1,0:T(8,128)} %copy-done.3) | copy-start | bytes 9437188
  323.5 425.9 %reduce-scatter.5.cloned.1.call-start = ((), (), s32[]{:S(2)}) async-start(), calls=%async_computation.12 | async-start | bytes 7962624 | tf_op jit(solution)/shard_map/reduce_scatter | solution.py:233
  390.0 525.6 %reduce-scatter.9.cloned.1.call-start = ((), (), s32[]{:S(2)}) async-start(), calls=%async_computation.14 | async-start | bytes 10616832 | tf_op jit(solution)/shard_map/reduce_scatter | solution.py:240
  401.0 681.1 %reduce-scatter.11.cloned.1.call-start = ((), (), s32[]{:S(2)}) async-start(), calls=%async_computation.15 | async-start | bytes 10616832 | tf_op jit(solution)/shard_map/reduce_scatter | solution.py:242
  412.6 724.0 %all-reduce.23.cloned.1.call-start = ((), (), s32[]{:S(2)}) async-start(), calls=%async_computation.16 | async-start | bytes 3538944 | tf_op jit(solution)/shard_map/psum | solution.py:248
  416.1 18.4 %copy-start.15 = (f32[200,768]{1,0:T(8,128)}, f32[200,768]{1,0:T(8,128)S(1)}, u32[]{:S(2)}) copy-start(f32[200,768]{1,0:T(8,128)S(1)} %reshape.245) | copy-start | bytes 1843204
  456.3 11.1 slice-start.2
  456.3 11.2 slice-start.4
  456.4 11.1 slice-start.3
  456.4 11.1 slice-start.5
  (40 other events, 184.3 us)
Sparse Core Ops, SparseCore 0:
  10.2 65.5 all-gather.10
  78.0 39.6 all-gather.12
  119.8 78.0 all-gather.14
  200.0 78.0 all-gather.16
  280.1 63.7 all-gather.18
  345.9 39.6 all-gather.20
  387.8 78.1 all-gather.22
  468.2 78.0 all-gather.24
  549.7 67.2 reduce-scatter.6
  620.5 128.8 reduce-scatter.4
  753.4 162.1 reduce-scatter.8
  919.5 162.5 reduce-scatter.10
  1086.0 46.6 all-reduce.22
where the time goes:
time: 1160 us; the launch traced here: 1150 us
  waiting for transfers between devices  681 us (59%)
  matrix products  189 us (16%)
  local copies, waits for them, and re-layouts  108 us (9%)
  blocking collectives  107 us (9%)
  other arithmetic  46.8 us (4%)
  between operations  17 us (1%)
    reduce_scatter x1, waiting for transfers between devices, per_device(): lax.psum_scatter(grad_fc2, 'fsdp', scatter_dimension=0, tiled=True)  164 us
    reduce_scatter x1, waiting for transfers between devices, per_device(): lax.psum_scatter(grad_fc1, 'fsdp', scatter_dimension=0, tiled=True)  164 us
    reduce_scatter x1, waiting for transfers between devices, per_device(): lax.psum_scatter(grad_qkv, 'fsdp', scatter_dimension=0, tiled=True)  131 us
    all_gather x1, waiting for transfers between devices, per_device(): lax.all_gather(image_fc2, 'fsdp', axis=0, tiled=True)  72.3 us
    reduce_scatter x1, waiting for transfers between devices, per_device(): lax.psum_scatter(grad_w_out, 'fsdp', scatter_dimension=0, tiled=True)  59.2 us
    unnamed x2, blocking collectives  55.4 us
    all_gather x1, waiting for transfers between devices, per_device(): lax.all_gather(w_fc2, 'fsdp', axis=0, tiled=True)  42.2 us
    all_gather x1, waiting for transfers between devices, per_device(): lax.all_gather(w_fc1, 'fsdp', axis=0, tiled=True)  39.6 us
  transfers between devices with their start and end apart: 13, of which 8 were waited for; matrix products, arithmetic and copies ran while one was open for 28% of the time, Pallas kernels for 0%

commit v1 on v0

v1 whole, which is shorter than its diff:
```python
from functools import partial

import jax
import jax.numpy as jnp
from jax import lax
from jax.experimental import pallas as pl
from jax.experimental.pallas import tpu as pltpu
from jax.sharding import PartitionSpec as P

HEADS = 12
EPSILON = 1e-06
LANES = 128
TILE = 256
MIB = 1024 * 1024
F32 = jnp.float32
BF16 = jnp.bfloat16

LN1_GAIN, LN1_BIAS, Q_BIAS, V_BIAS, OUT_BIAS, LN2_GAIN, LN2_BIAS, FC2_BIAS = range(8)
IMAGE_GAIN_ONE, IMAGE_GAIN_TWO, FC1_BIAS = 8, 9, 10
VECTOR_ROWS = 16


def dot_nn(a, b):
    return lax.dot_general(a, b, (((1,), (0,)), ((), ())), preferred_element_type=F32)


def dot_nt(a, b):
    return lax.dot_general(a, b, (((1,), (1,)), ((), ())), preferred_element_type=F32)


def dot_tn(a, b):
    return lax.dot_general(a, b, (((0,), (0,)), ((), ())), preferred_element_type=F32)


def call(body, name, flops, moved, **kwargs):
    return pl.pallas_call(
        body,
        name=name,
        compiler_params=pltpu.CompilerParams(vmem_limit_bytes=60 * MIB),
        cost_estimate=pl.CostEstimate(
            flops=int(flops), bytes_accessed=int(moved), transcendentals=0
        ),
        **kwargs,
    )


class Part:
    def __init__(self, name, start, width, folds):
        self.name, self.start, self.width, self.folds = name, start, width, folds


def pack_parts(shapes, n_fsdp):
    parts, at = {}, 0
    for name, (rows, columns), model in shapes:
        folds = rows // model
        parts[name] = Part(name, at, columns // 2, folds)
        at += folds * (columns // 2)
    return parts, at


def own_piece(matrix, folds, x, core):
    rows, columns = matrix.shape
    half = rows // 2
    piece = lax.dynamic_slice(matrix, (x * half, core * (columns // 2)), (half, columns // 2))
    if folds > 1:
        step = half // folds
        piece = jnp.concatenate([piece[k * step : (k + 1) * step] for k in range(folds)], axis=1)
    return piece


class Whole:
    def __init__(self, arrays):
        self.arrays = arrays

    def operands(self, names):
        return [self.arrays[name] for name in names]

    def start(self, refs, place, names, targets, semaphores):
        for ref, name in zip(refs, names):
            pltpu.make_async_copy(ref, targets[name], semaphores[name]).start()


def start_piece(source, parts, names, targets, semaphores, f, x, core):
    for name in names:
        part = parts[name]
        height = source.shape[0]
        first = f * (2 * part.folds * height) + x * (part.folds * height)
        for fold in range(part.folds):
            columns = part.start + fold * part.width
            pltpu.make_async_copy(
                source.at[:, pl.ds(columns, part.width)],
                targets[name].at[
                    pl.ds(pl.multiple_of(first + fold * height, 16), height),
                    pl.ds(pl.multiple_of(core * part.width, LANES), part.width),
                ],
                semaphores[name],
            ).start()


class Relative:
    def __init__(self, parts, buffers):
        self.parts, self.buffers = parts, buffers

    def operands(self, names):
        return [array for array, _ in self.buffers]

    def start(self, refs, place, names, targets, semaphores):
        f, x, core = place
        for ref, (_, (high, dy, dx, dc)) in zip(refs, self.buffers):
            for low in range(2):
                start_piece(
                    ref.at[low],
                    self.parts,
                    names,
                    targets,
                    semaphores,
                    f ^ (dy + 2 * (2 * high + low)),
                    x ^ dx,
                    core ^ dc,
                )


class Listed:
    def __init__(self, parts, array):
        self.parts, self.array = parts, array

    def operands(self, names):
        return [self.array]

    def start(self, refs, place, names, targets, semaphores):
        (ref,) = refs

        def step(i, carry):
            start_piece(
                ref.at[i], self.parts, names, targets, semaphores, i // 4, (i // 2) % 2, i % 2
            )
            return carry

        lax.fori_loop(0, ref.shape[0], step, 0)


class Loader:
    def __init__(self, wanted, shapes):
        self.wanted, self.shapes = wanted, shapes
        self.names = [name for _, names in wanted for name in names]
        self.arrays = [a for source, names in wanted for a in source.operands(names)]
        self.specs = [pl.BlockSpec(memory_space=pl.ANY)] * len(self.arrays)
        self.scratch = [pltpu.VMEM(shapes[name], BF16) for name in self.names] + [
            pltpu.SemaphoreType.DMA((len(self.names),))
        ]
        self.bytes = sum(2 * shapes[name][0] * shapes[name][1] for name in self.names)

    def bind(self, refs, scratch, place_ref):
        self.refs = refs
        self.targets = dict(zip(self.names, scratch))
        self.semaphores = {name: scratch[-1].at[i] for i, name in enumerate(self.names)}
        self.place = (place_ref[0], place_ref[1], place_ref[2])
        return self

    def start(self):
        at = 0
        for source, names in self.wanted:
            count = len(source.operands(names))
            source.start(
                self.refs[at : at + count], self.place, names, self.targets, self.semaphores
            )
            at += count

    def wait(self, name):
        target = self.targets[name]
        pltpu.make_async_copy(target, target, self.semaphores[name]).wait()


def normed(values, gain, shift):
    centre = values - jnp.mean(values, axis=-1, keepdims=True)
    spread = lax.rsqrt(jnp.mean(centre * centre, axis=-1, keepdims=True) + EPSILON)
    return centre * spread * gain + shift


def norm_back(values, gain, grad):
    centre = values - jnp.mean(values, axis=-1, keepdims=True)
    spread = lax.rsqrt(jnp.mean(centre * centre, axis=-1, keepdims=True) + EPSILON)
    scaled = centre * spread
    grad_gain = jnp.sum(grad * scaled, axis=0, keepdims=True)
    grad_shift = jnp.sum(grad, axis=0, keepdims=True)
    inner = grad * gain
    inner = inner - jnp.mean(inner, axis=-1, keepdims=True) - scaled * jnp.mean(
        inner * scaled, axis=-1, keepdims=True
    )
    return inner * spread, grad_gain, grad_shift


def lane_sides(scale=1.0):
    lane = lax.broadcasted_iota(jnp.int32, (LANES, LANES), 1)
    left = jnp.where(lane < LANES // 2, scale, 0.0)
    return left.astype(BF16), (scale - left).astype(BF16)


def by_head(values, sides):
    return jnp.concatenate([values * sides[0], values * sides[1]], axis=0)


def attention(queries, keys, values, allowed, sides, key_sides):
    scores = dot_nt(queries, by_head(keys, key_sides))
    weights = []
    for head in range(2):
        own = jnp.where(allowed, scores[:, head * LANES : (head + 1) * LANES], -1e30)
        raised = jnp.exp(own - jnp.max(own, axis=-1, keepdims=True))
        weights.append(raised / jnp.sum(raised, axis=-1, keepdims=True))
    weights = jnp.concatenate(weights, axis=1).astype(BF16)
    return weights, dot_nn(weights, by_head(values, sides))


def gelu_both(values):
    below = 0.5 + 0.5 * lax.erf(values * 0.7071067811865476)
    bell = jnp.exp(values * values * -0.5) * 0.3989422804014327
    return values * below, below + values * bell


def text_attend_body(loader, n_sources, width, place, x_ref, ids_ref, vec_ref, *rest):
    sources, rest = rest[:n_sources], rest[n_sources:]
    normed_ref, joined_ref, mixed_ref, weights_ref = rest[:4]
    load = loader.bind(sources, rest[4:], place)

    @pl.when(pl.program_id(0) == 0)
    def _():
        load.start()
        load.wait("qkv")

    w_qkv = load.targets["qkv"]
    values = x_ref[...].astype(F32)
    norm_one = normed(
        values, vec_ref[LN1_GAIN : LN1_GAIN + 1, :], vec_ref[LN1_BIAS : LN1_BIAS + 1, :]
    ).astype(BF16)
    normed_ref[...] = norm_one
    for third, bias in enumerate((Q_BIAS, None, V_BIAS)):
        columns = slice(third * width, (third + 1) * width)
        product = dot_nn(norm_one, w_qkv[:, columns])
        if bias is not None:
            product = product + vec_ref[bias : bias + 1, :]
        joined_ref[:, columns] = product.astype(BF16)
    sides, key_sides = lane_sides(), lane_sides((width // HEADS) ** -0.5)
    for part in range(x_ref.shape[0] // LANES):
        rows = slice(part * LANES, (part + 1) * LANES)
        ids = jnp.broadcast_to(ids_ref[part], (LANES, LANES))
        allowed = ids == ids.T
        for pair in range(width // LANES):
            one = slice(pair * LANES, (pair + 1) * LANES)
            two = slice(width + pair * LANES, width + (pair + 1) * LANES)
            three = slice(2 * width + pair * LANES, 2 * width + (pair + 1) * LANES)
            weights, mixed = attention(
                joined_ref[rows, one],
                joined_ref[rows, two],
                joined_ref[rows, three],
                allowed,
                sides,
                key_sides,
            )
            weights_ref[part, pair] = weights
            mixed_ref[rows, one] = mixed.astype(BF16)


def text_hidden_body(loader, n_sources, place, x_ref, mixed_ref, vec_ref, fc1_bias_ref, *rest):
    sources, rest = rest[:n_sources], rest[n_sources:]
    hidden_ref, norm_two_ref, active_ref, slope_ref = rest[:4]
    load = loader.bind(sources, rest[4:], place)

    @pl.when(pl.program_id(0) == 0)
    def _():
        load.start()
        load.wait("out")
        load.wait("fc1")

    w_out, w_fc1 = load.targets["out"], load.targets["fc1"]
    hidden = (
        x_ref[...].astype(F32)
        + dot_nn(mixed_ref[...], w_out[...])
        + vec_ref[OUT_BIAS : OUT_BIAS + 1, :]
    )
    hidden_ref[...] = hidden
    norm_two = normed(
        hidden, vec_ref[LN2_GAIN : LN2_GAIN + 1, :], vec_ref[LN2_BIAS : LN2_BIAS + 1, :]
    ).astype(BF16)
    norm_two_ref[...] = norm_two
    step = hidden.shape[1]
    for k in range(w_fc1.shape[1] // step):
        columns = slice(k * step, (k + 1) * step)
        pre_act = dot_nn(norm_two, w_fc1[:, columns]) + fc1_bias_ref[:, columns]
        active, slope = gelu_both(pre_act)
        active_ref[:, columns] = active.astype(BF16)
        slope_ref[:, columns] = slope.astype(BF16)


def text_back_body(loader, n_sources, place, g_ref, hidden_ref, active_ref, slope_ref, vec_ref, *rest):
    sources, rest = rest[:n_sources], rest[n_sources:]
    out_ref, pre_ref, d_hidden_ref, dy1_ref, d_mixed_ref, sums_ref, wide_ref = rest[:7]
    load = loader.bind(sources, rest[7:], place)
    first = pl.program_id(0) == 0

    @pl.when(first)
    def _():
        load.start()
        for name in load.names:
            load.wait(name)
        sums_ref[...] = jnp.zeros_like(sums_ref)
        wide_ref[...] = jnp.zeros_like(wide_ref)

    w_out, w_fc1, w_fc2 = (load.targets[name] for name in ("out", "fc1", "fc2"))
    g = g_ref[...]
    hidden = hidden_ref[...]
    out_ref[...] = (
        hidden + dot_nn(active_ref[...], w_fc2[...]) + vec_ref[FC2_BIAS : FC2_BIAS + 1, :]
    ).astype(BF16)
    step = hidden.shape[1]
    d_norm = jnp.zeros(hidden.shape, F32)
    for k in range(w_fc1.shape[1] // step):
        columns = slice(k * step, (k + 1) * step)
        d_pre = dot_nt(g, w_fc2[columns, :]) * slope_ref[:, columns].astype(F32)
        low = d_pre.astype(BF16)
        pre_ref[:, columns] = low
        wide_ref[0:1, columns] += jnp.sum(low.astype(F32), axis=0, keepdims=True)
        d_norm = d_norm + dot_nt(low, w_fc1[:, columns])
    part, gain, shift = norm_back(hidden, vec_ref[LN2_GAIN : LN2_GAIN + 1, :], d_norm)
    d_hidden = g.astype(F32) + part
    d_hidden_ref[...] = d_hidden
    dy1 = d_hidden.astype(BF16)
    dy1_ref[...] = dy1
    d_mixed_ref[...] = dot_nt(dy1, w_out[...]).astype(BF16)
    sums_ref[LN2_GAIN : LN2_GAIN + 1, :] += gain
    sums_ref[LN2_BIAS : LN2_BIAS + 1, :] += shift
    sums_ref[OUT_BIAS : OUT_BIAS + 1, :] += jnp.sum(dy1.astype(F32), axis=0, keepdims=True)
    sums_ref[FC2_BIAS : FC2_BIAS + 1, :] += jnp.sum(g.astype(F32), axis=0, keepdims=True)


def text_unjoin_body(
    loader, n_sources, width, place, x_ref, joined_ref, weights_ref, d_mixed_ref, d_hidden_ref, vec_ref, *rest
):
    sources, rest = rest[:n_sources], rest[n_sources:]
    d_joined_ref, grad_ref, sums_ref = rest[:3]
    load = loader.bind(sources, rest[3:], place)

    @pl.when(pl.program_id(0) == 0)
    def _():
        load.start()
        load.wait("qkv")
        sums_ref[...] = jnp.zeros_like(sums_ref)

    w_qkv = load.targets["qkv"]
    scale = (width // HEADS) ** -0.5
    sides, key_sides = lane_sides(), lane_sides(scale)
    left = lax.broadcasted_iota(jnp.int32, (LANES, LANES), 1) < LANES // 2
    for part in range(x_ref.shape[0] // LANES):
        rows = slice(part * LANES, (part + 1) * LANES)
        for pair in range(width // LANES):
            one = slice(pair * LANES, (pair + 1) * LANES)
            two = slice(width + pair * LANES, width + (pair + 1) * LANES)
            three = slice(2 * width + pair * LANES, 2 * width + (pair + 1) * LANES)
            low = weights_ref[part, pair]
            d_mixed = d_mixed_ref[rows, one]
            d_weights = dot_nt(d_mixed, by_head(joined_ref[rows, three], sides))
            d_scores = []
            for head in range(2):
                lanes = slice(head * LANES, (head + 1) * LANES)
                own, grad = low[:, lanes].astype(F32), d_weights[:, lanes]
                total = jnp.sum(grad * own, axis=-1, keepdims=True)
                total = total / jnp.sum(own, axis=-1, keepdims=True)
                d_scores.append(own * (grad - total))
            d_scores = jnp.concatenate(d_scores, axis=1).astype(BF16)
            d_joined_ref[rows, one] = dot_nn(
                d_scores, by_head(joined_ref[rows, two], key_sides)
            ).astype(BF16)
            d_keys = dot_tn(d_scores, joined_ref[rows, one]) * scale
            d_joined_ref[rows, two] = jnp.where(left, d_keys[:LANES], d_keys[LANES:]).astype(BF16)
            d_values = dot_tn(low, d_mixed)
            d_joined_ref[rows, three] = jnp.where(
                left, d_values[:LANES], d_values[LANES:]
            ).astype(BF16)
    d_joined = d_joined_ref[...]
    d_norm = dot_nt(d_joined, w_qkv[...])
    part, gain, shift = norm_back(
        x_ref[...].astype(F32), vec_ref[LN1_GAIN : LN1_GAIN + 1, :], d_norm
    )
    grad_ref[...] = d_hidden_ref[...] + part
    sums_ref[LN1_GAIN : LN1_GAIN + 1, :] += gain
    sums_ref[LN1_BIAS : LN1_BIAS + 1, :] += shift
    for row, third in ((Q_BIAS, 0), (V_BIAS, 2)):
        columns = d_joined_ref[:, third * width : (third + 1) * width].astype(F32)
        sums_ref[row : row + 1, :] += jnp.sum(columns, axis=0, keepdims=True)


def image_body(loader, n_sources, width, tokens, padded, place, x_ref, vec_ref, *rest):
    sources, rest = rest[:n_sources], rest[n_sources:]
    out_ref, joined_ref, mixed_ref, hidden_ref = rest[:4]
    load = loader.bind(sources, rest[4:], place)
    load.start()
    values = x_ref[...].astype(F32)
    norm_one = normed(values, vec_ref[IMAGE_GAIN_ONE : IMAGE_GAIN_ONE + 1, :], 0.0).astype(BF16)
    load.wait("qkv")
    w_qkv = load.targets["qkv"]
    for third in range(3):
        columns = slice(third * width, (third + 1) * width)
        joined_ref[:, columns] = dot_nn(norm_one, w_qkv[:, columns]).astype(BF16)
    sides, key_sides = lane_sides(), lane_sides((width // HEADS) ** -0.5)
    row = lax.broadcasted_iota(jnp.int32, (LANES, LANES), 0)
    column = lax.broadcasted_iota(jnp.int32, (LANES, LANES), 1)
    allowed = (row // padded == column // padded) & (column % padded < tokens)
    for part in range(x_ref.shape[0] // LANES):
        rows = slice(part * LANES, (part + 1) * LANES)
        for pair in range(width // LANES):
            one = slice(pair * LANES, (pair + 1) * LANES)
            two = slice(width + pair * LANES, width + (pair + 1) * LANES)
            three = slice(2 * width + pair * LANES, 2 * width + (pair + 1) * LANES)
            _, mixed = attention(
                joined_ref[rows, one],
                joined_ref[rows, two],
                joined_ref[rows, three],
                allowed,
                sides,
                key_sides,
            )
            mixed_ref[rows, one] = mixed.astype(BF16)
    load.wait("out")
    hidden = values + dot_nn(mixed_ref[...], load.targets["out"][...])
    norm_two = normed(hidden, vec_ref[IMAGE_GAIN_TWO : IMAGE_GAIN_TWO + 1, :], 0.0).astype(BF16)
    hidden_ref[...] = hidden
    load.wait("fc1")
    load.wait("fc2")
    w_fc1, w_fc2 = load.targets["fc1"], load.targets["fc2"]
    for k in range(w_fc1.shape[1] // width):
        columns = slice(k * width, (k + 1) * width)
        pre_act = dot_nn(norm_two, w_fc1[:, columns])
        active = (pre_act * (0.5 + 0.5 * lax.erf(pre_act * 0.7071067811865476))).astype(BF16)
        hidden_ref[...] += dot_nn(active, w_fc2[columns, :])
    out_ref[...] = hidden_ref[...].astype(BF16)


SLOTS = 16


def slot_place(slot, f, x):
    dy, dx, dz = slot // 8, (slot // 4) % 2, slot % 4
    return f ^ (dy + 2 * dz), x ^ dx


def grad_columns_body(place, left_ref, own_in, other_in, own_out, other_out, turned, total):
    @pl.when(pl.program_id(0) == 0)
    def _():
        turned[...] = left_ref[...].T

    height = own_out.shape[1]
    for right, out in ((other_in, other_out), (own_in, own_out)):
        total[...] = dot_nn(turned[...], right[...])
        for slot in range(SLOTS):
            f, x = slot_place(slot, place[0], place[1])
            rows = pl.ds(pl.multiple_of((f * 2 + x) * height, 16), height)
            out[slot] = total[rows, :].astype(BF16)


def grad_columns(place, left, right, name):
    tokens, model = left.shape
    columns = right.shape[1]
    width = columns // 2
    steps = width // 384
    block = width // steps
    height = model // SLOTS

    def own_block(j, place):
        return (0, place[2] * steps + j)

    def other_block(j, place):
        return (0, (1 - place[2]) * steps + j)

    out = jax.ShapeDtypeStruct((SLOTS, height, width), BF16)
    return call(
        grad_columns_body,
        name,
        2 * tokens * model * columns,
        2 * tokens * (model + columns) + 2 * model * columns,
        grid_spec=pltpu.PrefetchScalarGridSpec(
            num_scalar_prefetch=1,
            grid=(steps,),
            in_specs=[
                pl.BlockSpec((tokens, model), lambda j, place: (0, 0)),
                pl.BlockSpec((tokens, block), own_block),
                pl.BlockSpec((tokens, block), other_block),
            ],
            out_specs=[pl.BlockSpec((SLOTS, height, block), lambda j, place: (0, 0, j))] * 2,
            scratch_shapes=[pltpu.VMEM((model, tokens), BF16), pltpu.VMEM((model, block), F32)],
        ),
        out_shape=(out, out),
    )(place, left, right, right)


def grad_rows_body(place, left_ref, right_ref, own_out, other_out):
    total = dot_tn(left_ref[...], right_ref[...])
    half_rows, half_columns = total.shape[0] // 2, total.shape[1] // 2
    height = own_out.shape[3]
    first_x, first_core = place[1] == 0, place[2] == 0
    sides = (total[:, :half_columns], total[:, half_columns:])
    own = jnp.where(first_core, sides[0], sides[1]).astype(BF16)
    other = jnp.where(first_core, sides[1], sides[0]).astype(BF16)
    for value, out in ((other, other_out), (own, own_out)):
        ends = (value[:half_rows], value[half_rows:])
        for dx in range(2):
            rows = jnp.where(first_x, ends[dx], ends[1 - dx])
            for fold in range(half_rows // height):
                out[0, dx, 0, :, fold * half_columns : (fold + 1) * half_columns] = rows[
                    fold * height : (fold + 1) * height
                ]


def grad_rows(place, left, right, n_fsdp, name):
    tokens, columns = right.shape
    rows = left.shape[1] // n_fsdp
    folds = left.shape[1] // columns
    height, width = rows // (2 * folds), folds * columns // 2

    def left_block(i, place):
        return (0, place[0] ^ (i // 4 + 2 * (i % 4)))

    out = jax.ShapeDtypeStruct((2, 2, 4, height, width), BF16)
    own, other = call(
        grad_rows_body,
        name,
        2 * tokens * left.shape[1] * columns,
        2 * tokens * (left.shape[1] + columns) + 2 * left.shape[1] * columns,
        grid_spec=pltpu.PrefetchScalarGridSpec(
            num_scalar_prefetch=1,
            grid=(n_fsdp,),
            in_specs=[
                pl.BlockSpec((tokens, rows), left_block),
                pl.BlockSpec((tokens, columns), lambda i, place: (0, 0)),
            ],
            out_specs=[
                pl.BlockSpec((1, 2, 1, height, width), lambda i, place: (i // 4, 0, i % 4, 0, 0))
            ]
            * 2,
        ),
        out_shape=(out, out),
    )(place, left, right)
    return own.reshape(SLOTS, height, width), other.reshape(SLOTS, height, width)


def add_pairs_body(n_pairs, *refs):
    ins, outs = refs[: 2 * n_pairs], refs[2 * n_pairs :]
    at = 0
    for own, came in zip(ins[0::2], ins[1::2]):
        width = own.shape[2]
        value = (own[...].astype(F32) + came[...].astype(F32)).astype(BF16)
        for i, out in enumerate(outs):

            @pl.when(pl.program_id(0) == i)
            def _():
                out[:, :, at : at + width] = value

        at += width


def add_pairs(pairs, name):
    slots, height, _ = pairs[0][0].shape
    steps = slots // 2
    width = sum(own.shape[2] for own, _ in pairs)
    out = jax.ShapeDtypeStruct((2, height, width), BF16)
    return call(
        partial(add_pairs_body, len(pairs)),
        name,
        slots * height * width,
        6 * slots * height * width,
        grid=(steps,),
        in_specs=[
            pl.BlockSpec((2, height, array.shape[2]), lambda i: (i, 0, 0))
            for pair in pairs
            for array in pair
        ],
        out_specs=[pl.BlockSpec((2, height, width), lambda i: (0, 0, 0))] * steps,
        out_shape=[out] * steps,
    )(*[array for pair in pairs for array in pair])


def swap(value, axis, bit):
    size = lax.axis_size(axis)
    return lax.ppermute(value, axis, [(i, i ^ bit) for i in range(size)])


def gather_pieces(own):
    s0 = jnp.stack([own, swap(own, "fsdp", 2)])
    s1 = swap(s0, "fsdp", 4)
    y0, x0 = swap(s0, "fsdp", 1), swap(s0, "dp", 2)
    y1, x1 = swap(s1, "fsdp", 1), swap(s1, "dp", 2)
    d0, d1 = swap(y0, "dp", 2), swap(x1, "fsdp", 1)
    here = [
        (s0, (0, 0, 0)),
        (s1, (1, 0, 0)),
        (y0, (0, 1, 0)),
        (y1, (1, 1, 0)),
        (x0, (0, 0, 1)),
        (x1, (1, 0, 1)),
        (d0, (0, 1, 1)),
        (d1, (1, 1, 1)),
    ]
    return [(a, at + (0,)) for a, at in here] + [(swap(a, "dp", 1), at + (1,)) for a, at in here]


def plus(a, b):
    return (a.astype(F32) + b.astype(F32)).astype(a.dtype)


def reduce_pieces(pairs, name):
    came = [(own, swap(other, "dp", 1)) for own, other in pairs]
    s0, s1, x0, x1, y0, y1, d0, d1 = add_pairs(came, name)
    y0 = plus(y0, swap(d0, "dp", 2))
    x1 = plus(x1, swap(d1, "fsdp", 1))
    x0, y1 = swap(x0, "dp", 2), swap(y1, "fsdp", 1)
    x1, y0 = swap(x1, "dp", 2), swap(y0, "fsdp", 1)
    s1 = (s1.astype(F32) + x1.astype(F32) + y1.astype(F32)).astype(BF16)
    s0 = s0.astype(F32) + x0.astype(F32) + y0.astype(F32)
    came = swap(s1, "fsdp", 4)
    send = (s0[1] + came[1].astype(F32)).astype(BF16)
    keep = s0[0] + came[0].astype(F32)
    total = (keep + swap(send, "fsdp", 2).astype(F32)).astype(BF16)
    both = jnp.stack([total, swap(total, "dp", 2)])
    return both, swap(both, "dp", 1)


def unpack(both, other, x, core, start, width, folds):
    def rows(pieces):
        pieces = pieces[:, :, start : start + folds * width]
        pieces = jnp.where(x == 0, pieces, pieces[::-1])
        height = pieces.shape[1]
        pieces = pieces.reshape(2, height, folds, width).transpose(0, 2, 1, 3)
        return pieces.reshape(2 * folds * height, width)

    one, two = rows(both).astype(F32), rows(other).astype(F32)
    first = core == 0
    return jnp.concatenate([jnp.where(first, one, two), jnp.where(first, two, one)], axis=1)


def gather_vectors(own, f):
    bits = lax.axis_size("fsdp").bit_length() - 1
    order = [2, 4, 1] if bits == 3 else [1 << b for b in range(bits)]
    held = own
    for bit in order:
        held = jnp.stack([held, swap(held, "fsdp", bit)])
    for axis, bit in enumerate(reversed(order)):
        held = jnp.where((f & bit) != 0, jnp.flip(held, axis), held)
    wanted = sorted(range(bits), key=lambda axis: -order[::-1][axis])
    held = held.transpose(bits, *wanted, bits + 1)
    return held.reshape(own.shape[0], -1)


def reduce_vectors(sums, f):
    n = lax.axis_size("fsdp")
    rows = sums.shape[0]
    held = sums.reshape(rows, n, -1).transpose(1, 0, 2)
    bit = n // 2
    while bit:
        halves = held.reshape(2, bit, *held.shape[1:])
        upper = (f & bit) != 0
        send = jnp.where(upper, halves[0], halves[1])
        keep = jnp.where(upper, halves[1], halves[0])
        held = keep + swap(send, "fsdp", bit)
        bit //= 2
    held = held[0]
    bit = 1
    while bit < lax.axis_size("dp"):
        held = held + swap(held, "dp", bit)
        bit *= 2
    return held


def per_device(
    text_in,
    text_segments,
    text_cotangent,
    image_in,
    ln1_gain,
    ln1_bias,
    w_qkv,
    q_bias,
    v_bias,
    w_out,
    out_bias,
    ln2_gain,
    ln2_bias,
    w_fc1,
    fc1_bias,
    w_fc2,
    fc2_bias,
    image_norms,
    image_qkv,
    image_proj,
    image_fc1,
    image_fc2,
):
    n_fsdp, n_dp = lax.axis_size("fsdp"), lax.axis_size("dp")
    batch_rows, length, model = text_in.shape
    hidden_units = w_fc1.shape[1]
    tokens = batch_rows * length
    folds = hidden_units // model
    f, replica = lax.axis_index("fsdp"), lax.axis_index("dp")
    x, core = replica // 2, replica % 2
    place = jnp.stack([f, x, core]).astype(jnp.int32)
    shard = model // n_fsdp
    by_pieces = n_fsdp == 8 and n_dp == 4 and shard % 32 == 0

    shapes = {
        "qkv": (model, 3 * model),
        "out": (model, model),
        "fc1": (model, hidden_units),
        "fc2": (hidden_units, model),
    }
    text = {"qkv": w_qkv, "out": w_out, "fc1": w_fc1, "fc2": w_fc2}
    image = {"qkv": image_qkv, "out": image_proj, "fc1": image_fc1, "fc2": image_fc2}

    def packed(matrices, names):
        parts, _ = pack_parts([(name, shapes[name], model) for name in names], n_fsdp)
        return parts, jnp.concatenate(
            [own_piece(matrices[name], parts[name].folds, x, core) for name in names], axis=1
        )

    vectors = jnp.concatenate(
        [
            jnp.stack(
                [ln1_gain, ln1_bias, q_bias, v_bias, out_bias, ln2_gain, ln2_bias, fc2_bias]
            ),
            image_norms,
            fc1_bias.reshape(folds, shard),
        ]
    )
    vectors = jnp.pad(vectors, ((0, VECTOR_ROWS - vectors.shape[0]), (0, 0)))
    if by_pieces:
        parts, own = packed(text, ("qkv",))
        text_first = Relative(parts, gather_pieces(own))
        vectors = gather_vectors(vectors, f).astype(F32)
        parts, own = packed(text, ("out", "fc1", "fc2"))
        text_rest = Listed(parts, lax.all_gather(own, ("fsdp", "dp")))
        parts, own = packed(image, ("qkv", "out", "fc1", "fc2"))
        image_source = Listed(parts, lax.all_gather(own, ("fsdp", "dp")))
    else:
        vectors = lax.all_gather(vectors, "fsdp", axis=1, tiled=True).astype(F32)
        gathered = {n: lax.all_gather(a, "fsdp", axis=0, tiled=True) for n, a in text.items()}
        text_first = text_rest = Whole(gathered)
        image_source = Whole(
            {n: lax.all_gather(a, "fsdp", axis=0, tiled=True) for n, a in image.items()}
        )
    fc1_vector = vectors[FC1_BIAS : FC1_BIAS + folds].reshape(folds, n_fsdp, shard)
    fc1_vector = fc1_vector.transpose(1, 0, 2).reshape(1, hidden_units)

    inflow = text_in.reshape(tokens, model)
    cotangent = text_cotangent.reshape(tokens, model)
    ids = text_segments + 16 * (lax.broadcasted_iota(jnp.int32, text_segments.shape, 0) % (LANES // length))
    ids = ids.astype(F32).reshape(tokens // LANES, 1, LANES)
    steps = tokens // TILE
    groups = TILE // LANES
    pairs = model // LANES

    def rows_of(width):
        return pl.BlockSpec((TILE, width), lambda i, place: (i, 0))

    def fixed(*shape):
        return pl.BlockSpec(shape, lambda i, place: (0,) * len(shape))

    def array(*shape, dtype=BF16):
        return jax.ShapeDtypeStruct(shape, dtype)

    weights_spec = pl.BlockSpec((groups, pairs, LANES, 2 * LANES), lambda i, place: (i, 0, 0, 0))
    vec_spec = fixed(VECTOR_ROWS, model)

    def run(body, loader, name, flops, moved, in_specs, out_specs, out_shape, operands, grid=(steps,), extra=()):
        return call(
            body,
            name,
            flops,
            moved + loader.bytes,
            grid_spec=pltpu.PrefetchScalarGridSpec(
                num_scalar_prefetch=1,
                grid=grid,
                in_specs=list(in_specs) + loader.specs,
                out_specs=out_specs,
                scratch_shapes=list(extra) + loader.scratch,
            ),
            out_shape=out_shape,
        )(place, *operands, *loader.arrays)

    square = 2 * tokens * model * model
    loader = Loader([(text_first, ["qkv"])], shapes)
    norm_one, joined, mixed, weights = run(
        partial(text_attend_body, loader, len(loader.arrays), model),
        loader,
        "text_attend",
        4 * square,
        tokens * model * 20,
        [rows_of(model), pl.BlockSpec((groups, 1, LANES), lambda i, place: (i, 0, 0)), vec_spec],
        [rows_of(model), rows_of(3 * model), rows_of(model), weights_spec],
        [
            array(tokens, model),
            array(tokens, 3 * model),
            array(tokens, model),
            array(tokens // LANES, pairs, LANES, 2 * LANES),
        ],
        (inflow, ids, vectors),
    )

    loader = Loader([(text_rest, ["out", "fc1"])], shapes)
    hidden, norm_two, active, slope = run(
        partial(text_hidden_body, loader, len(loader.arrays)),
        loader,
        "text_hidden",
        (1 + folds) * square,
        tokens * model * (10 + 4 * folds),
        [rows_of(model), rows_of(model), vec_spec, fixed(1, hidden_units)],
        [rows_of(model), rows_of(model), rows_of(hidden_units), rows_of(hidden_units)],
        [
            array(tokens, model, dtype=F32),
            array(tokens, model),
            array(tokens, hidden_units),
            array(tokens, hidden_units),
        ],
        (inflow, mixed, vectors, fc1_vector),
    )

    loader = Loader([(text_rest, ["out", "fc1", "fc2"])], shapes)
    text_out, d_pre, d_hidden, dy1, d_mixed, sums_two, sums_wide = run(
        partial(text_back_body, loader, len(loader.arrays)),
        loader,
        "text_back",
        (1 + 3 * folds) * square,
        tokens * model * (16 + 6 * folds),
        [rows_of(model), rows_of(model), rows_of(hidden_units), rows_of(hidden_units), vec_spec],
        [
            rows_of(model),
            rows_of(hidden_units),
            rows_of(model),
            rows_of(model),
            rows_of(model),
            fixed(8, model),
            fixed(8, hidden_units),
        ],
        [
            array(tokens, model),
            array(tokens, hidden_units),
            array(tokens, model, dtype=F32),
            array(tokens, model),
            array(tokens, model),
            array(8, model, dtype=F32),
            array(8, hidden_units, dtype=F32),
        ],
        (cotangent, hidden, active, slope, vectors),
    )

    loader = Loader([(text_first, ["qkv"])], shapes)
    d_joined, text_grad, sums_one = run(
        partial(text_unjoin_body, loader, len(loader.arrays), model),
        loader,
        "text_unjoin",
        5 * square,
        tokens * model * 28,
        [
            rows_of(model),
            rows_of(3 * model),
            weights_spec,
            rows_of(model),
            rows_of(model),
            vec_spec,
        ],
        [rows_of(3 * model), rows_of(model), fixed(8, model)],
        [
            array(tokens, 3 * model),
            array(tokens, model, dtype=F32),
            array(8, model, dtype=F32),
        ],
        (inflow, joined, weights, d_mixed, d_hidden, vectors),
    )

    images, image_tokens, _ = image_in.shape
    padded = -(-image_tokens // 64) * 64
    image_rows = jnp.pad(image_in, ((0, 0), (0, padded - image_tokens), (0, 0)))
    image_rows = image_rows.reshape(images * padded, model)
    loader = Loader([(image_source, ["qkv", "out", "fc1", "fc2"])], shapes)
    held = images * padded
    image_out = run(
        partial(image_body, loader, len(loader.arrays), model, image_tokens, padded),
        loader,
        "image_block",
        2 * held * model * model * (4 + 2 * folds),
        4 * held * model,
        [fixed(held, model), vec_spec],
        fixed(held, model),
        array(held, model),
        (image_rows, vectors),
        grid=(1,),
        extra=[
            pltpu.VMEM((held, 3 * model), BF16),
            pltpu.VMEM((held, model), BF16),
            pltpu.VMEM((held, model), F32),
        ],
    )
    image_out = image_out.reshape(images, padded, model)[:, :image_tokens]

    if by_pieces:
        two = grad_rows(place, active, cotangent, n_fsdp, "grad_fc2")
        got = reduce_pieces([two], "add_fc2")
        grad_fc2 = unpack(*got, x, core, 0, model // 2, folds)
        one = grad_columns(place, norm_two, d_pre, "grad_fc1")
        out = grad_columns(place, mixed, dy1, "grad_out")
        got = reduce_pieces([one, out], "add_fc1")
        grad_fc1 = unpack(*got, x, core, 0, hidden_units // 2, 1)
        grad_out = unpack(*got, x, core, hidden_units // 2, model // 2, 1)
        got = reduce_pieces([grad_columns(place, norm_one, d_joined, "grad_qkv")], "add_qkv")
        grad_qkv = unpack(*got, x, core, 0, 3 * model // 2, 1)
    else:

        def product(left, right):
            total = lax.psum_scatter(dot_tn(left, right), "fsdp", scatter_dimension=0, tiled=True)
            return lax.psum(total, "dp")

        grad_fc2 = product(active, cotangent)
        grad_fc1 = product(norm_two, d_pre)
        grad_out = product(mixed, dy1)
        grad_qkv = product(norm_one, d_joined)

    wide = sums_wide[0].reshape(n_fsdp, folds, shard).transpose(1, 0, 2).reshape(folds, model)
    sums = jnp.concatenate([sums_one + sums_two, wide])
    sums = reduce_vectors(sums, f)
    return (
        text_out.reshape(text_in.shape),
        image_out,
        text_grad.reshape(text_in.shape),
        sums[LN1_GAIN],
        sums[LN1_BIAS],
        grad_qkv,
        sums[Q_BIAS],
        sums[V_BIAS],
        grad_out,
        sums[OUT_BIAS],
        sums[LN2_GAIN],
        sums[LN2_BIAS],
        grad_fc1,
        sums[8 : 8 + folds].reshape(-1),
        grad_fc2,
        sums[FC2_BIAS],
    )


def solution(mesh):
    rows = P(("dp", "fsdp"), None, None)
    vector, matrix = P("fsdp"), P("fsdp", None)
    in_specs = (
        rows,
        P(("dp", "fsdp"), None),
        rows,
        rows,
        vector,
        vector,
        matrix,
        vector,
        vector,
        matrix,
        vector,
        vector,
        vector,
        matrix,
        vector,
        matrix,
        vector,
        P(None, "fsdp"),
        matrix,
        matrix,
        matrix,
        matrix,
    )
    out_specs = (
        rows,
        rows,
        rows,
        vector,
        vector,
        matrix,
        vector,
        vector,
        matrix,
        vector,
        vector,
        vector,
        matrix,
        vector,
        matrix,
        vector,
    )
    return jax.shard_map(
        per_device, mesh=mesh, in_specs=in_specs, out_specs=out_specs, check_vma=False
    )
```

time: 1160 us -> 421 us (0.36)
  waiting for transfers between devices: 681 us -> 128 us
  matrix products: 189 us -> 0 us
  Pallas kernels: 0 us -> 164 us
  blocking collectives: 107 us -> 0 us
  local copies, waits for them, and re-layouts: 108 us -> 25 us
  starting transfers between devices: 0.51 us -> 74.6 us
  other arithmetic: 46.8 us -> 9.93 us
    reduce_scatter x4 -> x0, waiting for transfers between devices: 518 us -> none  [the longest x1 164 us: per_device(): lax.psum_scatter(grad_fc2, 'fsdp', scatter_dimension=0, tiled=True)]
    dot_general x23 -> x0, matrix products: 187 us -> none  [the longest x1 37.9 us: forward_block(): jnp.dot(norm_two, w_fc1, preferred_element_type=jnp.float32) + fc1_bias]
    pallas_call x0 -> x12, Pallas kernels: none -> 164 us  [the longest x5 105 us: run(): call(body, name, flops, moved + loader.bytes, grid_spec=pltpu.PrefetchSca...]
    all_gather x8 -> x2, waiting for transfers between devices: 158 us -> 32.5 us  [the longest x1 32.5 us: per_device(): text_rest = Listed(parts, lax.all_gather(own, ('fsdp', 'dp')))]
    ppermute x0 -> x58, waiting for transfers between devices: none -> 95.1 us  [swap(): return lax.ppermute(value, axis, [(i, i ^ bit) for i in range(size)])]
    ppermute x0 -> x58, starting transfers between devices: none -> 74.5 us  [swap(): return lax.ppermute(value, axis, [(i, i ^ bit) for i in range(size)])]
    unnamed x2 -> x0, blocking collectives: 55.4 us -> none
    convert_element_type x11 -> x2, local copies, waits for them, and re-layouts: 49.8 us -> 0.8 us  [per_device(): vectors = gather_vectors(vectors, f).astype(F32)]
  transfers between devices with their start and end apart: 13 -> 60, of which waited for: 8 -> 25; matrix products, arithmetic and copies ran while one was open for 28% -> 5% of each run, Pallas kernels for 0% -> 36%
where the time goes in v1:
time: 421 us; the launch traced here: 416 us
  Pallas kernels  164 us (39%)
  waiting for transfers between devices  128 us (30%)
  starting transfers between devices  74.6 us (18%)
  local copies, waits for them, and re-layouts  25 us (6%)
  between operations  14.9 us (4%)
  other arithmetic  9.93 us (2%)
    pallas_call x5, Pallas kernels, run(): call(body, name, flops, moved + loader.bytes, grid_spec=pltpu.PrefetchSca...  105 us
    ppermute x58, waiting for transfers between devices, swap(): return lax.ppermute(value, axis, [(i, i ^ bit) for i in range(size)])  95.1 us
    ppermute x58, starting transfers between devices, swap(): return lax.ppermute(value, axis, [(i, i ^ bit) for i in range(size)])  74.5 us
    all_gather x1, waiting for transfers between devices, per_device(): text_rest = Listed(parts, lax.all_gather(own, ('fsdp', 'dp')))  32.5 us
    pallas_call x3, Pallas kernels, grad_columns(): call(grad_columns_body, name, 2 * tokens * model * columns, 2 * tokens *...  26.6 us
    pallas_call x3, Pallas kernels, add_pairs(): call(partial(add_pairs_body, len(pairs)), name, slots * height * width, 6...  20.3 us
    unnamed x109, local copies, waits for them, and re-layouts  16.4 us
    pallas_call x1, Pallas kernels, grad_rows(): call(grad_rows_body, name, 2 * tokens * left.shape[1] * columns, 2 * toke...  11.8 us
  transfers between devices with their start and end apart: 60, of which 25 were waited for; matrix products, arithmetic and copies ran while one was open for 5% of the time, Pallas kernels for 36%

profile of v1, /device:TPU:11, one launch (start us, length us, event | category | flops | bytes accessed | tf_op | source)
XLA Modules:
  0.0 415.9 jit_solution(13771791497927117832)
XLA Ops:
  35.7 6.9 %collective-permute-done.4.rest_1_ = bf16[2,48,1152]{2,1,0:T(8,128)(2,1)S(1)} collective-permute-done((bf16[2,48,1152]{2,1,0:T(8,128)(2,1)S(1)}, bf16[2,48,1152]{2,1,0:T(8,128)(2,1)S(1)}, u32[]{:S(2)}, u32[]{:S(2)}) %collective-permute-start.4) | collective-permute-done | bytes 221216 | tf_op jit(solution)/shard_map/ppermute | solution.py:582
  49.9 5.0 %collective-permute-start.15 = (bf16[2,48,1152]{2,1,0:T(8,128)(2,1)S(1)}, bf16[2,48,1152]{2,1,0:T(8,128)(2,1)S(1)}, u32[]{:S(2)}, u32[]{:S(2)}) collective-permute-start(bf16[2,48,1152]{2,1,0:T(8,128)(2,1)S(1)} %collective-permute-done.7.rest_4_), channel_id=1, source_target_pairs={{0,8},{8,0},{16,24},{24,16},{1,9},{9,1},{17,25},{25,17},{2,10},{10... | collective-permute-start | bytes 663560 | tf_op jit(solution)/shard_map/ppermute | solution.py:582
  65.0 17.1 %text_attend.1 = (bf16[1024,768]{1,0:T(8,128)(2,1)}, bf16[1024,2304]{1,0:T(8,128)(2,1)}, bf16[1024,768]{1,0:T(8,128)(2,1)}, bf16[8,6,128,256]{3,2,1,0:T(8,128)(2,1)}) custom-call(s32[3]{0:T(128)} %pad_add_fusion.place, bf16[1024,768]{1,0:T(8,128)(2,1)} %bitcast.140, f32[8,1,128]{2,1,0:T(1,128)} %reshape.146.ids_ref, ...), custom_call_target="tpu_custom_call" | custom-call | flops 4831838208 | bytes 19267584 | tf_op jit(solution)/shard_map/text_attend/pallas_call | solution.py:770
  82.1 32.5 %all-gather.5.cloned.1.call-done = bf16[1536,3456]{1,0:T(8,128)(2,1)} async-done(((bf16[48,3456]{1,0:T(8,128)(2,1)}), bf16[1536,3456]{1,0:T(8,128)(2,1)}) %all-gather.5.cloned.1.call-update) | async-done | bytes 10616848 | tf_op jit(solution)/shard_map/all_gather | solution.py:736
  114.6 19.3 %text_hidden.1 = (f32[1024,768]{1,0:T(8,128)}, bf16[1024,768]{1,0:T(8,128)(2,1)}, bf16[1024,3072]{1,0:T(8,128)(2,1)}, bf16[1024,3072]{1,0:T(8,128)(2,1)}) custom-call(s32[3]{0:T(128)} %pad_add_fusion.place, bf16[1024,768]{1,0:T(8,128)(2,1)} %bitcast.141, bf16[1024,768]{1,0:T(8,128)(2,1)} %get-tuple-element.66.mixed_ref.left_ref, ...), custom_call_target="tpu_custom_call" | custom-call | flops 6039797760 | bytes 26345472 | tf_op jit(solution)/shard_map/text_hidden/pallas_call | solution.py:770
  133.9 28.1 %text_back.1 = (bf16[1024,768]{1,0:T(8,128)(2,1)}, bf16[1024,3072]{1,0:T(8,128)(2,1)}, f32[1024,768]{1,0:T(8,128)}, bf16[1024,768]{1,0:T(8,128)(2,1)}, bf16[1024...) custom-call(s32[3]{0:T(128)} %pad_add_fusion.place, bf16[1024,768]{1,0:T(8,128)(2,1)} %bitcast.143, ...), custom_call_target="tpu_custom_call" | custom-call | flops 15703474176 | bytes 42074112 | tf_op jit(solution)/shard_map/text_back/pallas_call | solution.py:770
  163.0 26.7 %text_unjoin.1 = (bf16[1024,2304]{1,0:T(8,128)(2,1)}, f32[1024,768]{1,0:T(8,128)}, f32[8,768]{1,0:T(8,128)}) custom-call(s32[3]{0:T(128)} %pad_add_fusion.place, bf16[1024,768]{1,0:T(8,128)(2,1)} %bitcast.142, bf16[1024,2304]{1,0:T(8,128)(2,1)} %get-tuple-element.71.joined_ref, bf16[8,6,128,256]{3,2,1,0:T(8,128)(2,1)} %get-tuple-element.72.weights_ref, ...), custom_call_target="tpu_custom_call" | custom-call | flops 6039797760 | bytes 25559040 | tf_op jit(solution)/shard_map/text_unjoin/pallas_call | solution.py:770
  190.6 9.7 %grad_qkv.1 = (bf16[16,48,1152]{2,1,0:T(8,128)(2,1)}, bf16[16,48,1152]{2,1,0:T(8,128)(2,1)}) custom-call(s32[3]{0:T(128)} %pad_add_fusion.place, bf16[1024,768]{1,0:T(8,128)(2,1)} %get-tuple-element.79.left_ref, bf16[1024,2304]{1,0:T(8,128)(2,1)} %get-tuple-element.80.own_in.other_in, bf16[1024,2304]{1,0:T(8,128)(2,1)} %get-tuple-element.80.own_in.other_in), custom_call_target="tpu_custom_call" | custom-call | flops 3623878656 | bytes 9830400 | tf_op jit(solution)/shard_map/grad_qkv/pallas_call | solution.py:474
  208.1 11.8 %grad_fc2.1 = (bf16[2,2,4,48,1536]{4,3,2,1,0:T(8,128)(2,1)}, bf16[2,2,4,48,1536]{4,3,2,1,0:T(8,128)(2,1)}) custom-call(s32[3]{0:T(128)} %pad_add_fusion.place, bf16[1024,3072]{1,0:T(8,128)(2,1)} %get-tuple-element.68.active_ref.left_ref, bf16[1024,768]{1,0:T(8,128)(2,1)} %bitcast.144), custom_call_target="tpu_custom_call" | custom-call | flops 4831838208 | bytes 12582912 | tf_op jit(solution)/shard_map/grad_fc2/pallas_call | solution.py:522
  225.2 6.3 %add_qkv.1 = (bf16[2,48,1152]{2,1,0:T(8,128)(2,1)}, bf16[2,48,1152]{2,1,0:T(8,128)(2,1)}, bf16[2,48,1152]{2,1,0:T(8,128)(2,1)}, bf16[2,48,1152]{2,1,0:T(8,128)(2...) custom-call(bf16[16,48,1152]{2,1,0:T(8,128)(2,1)} %get-tuple-element, ...), custom_call_target="tpu_custom_call" | custom-call | flops 884736 | bytes 5308416 | tf_op jit(solution)/shard_map/add_qkv/pallas_call | solution.py:564
  232.6 11.5 %grad_fc1.1 = (bf16[16,48,1536]{2,1,0:T(8,128)(2,1)}, bf16[16,48,1536]{2,1,0:T(8,128)(2,1)}) custom-call(s32[3]{0:T(128)} %pad_add_fusion.place, bf16[1024,768]{1,0:T(8,128)(2,1)} %get-tuple-element.91.left_ref, bf16[1024,3072]{1,0:T(8,128)(2,1)} %get-tuple-element.92.own_in.other_in, bf16[1024,3072]{1,0:T(8,128)(2,1)} %get-tuple-element.92.own_in.other_in), custom_call_target="tpu_custom_call" | custom-call | flops 4831838208 | bytes 12582912 | tf_op jit(solution)/shard_map/grad_fc1/pallas_call | solution.py:474
  244.9 5.4 %grad_out.1 = (bf16[16,48,384]{2,1,0:T(8,128)(2,1)}, bf16[16,48,384]{2,1,0:T(8,128)(2,1)}) custom-call(s32[3]{0:T(128)} %pad_add_fusion.place, bf16[1024,768]{1,0:T(8,128)(2,1)} %get-tuple-element.66.mixed_ref.left_ref, bf16[1024,768]{1,0:T(8,128)(2,1)} %get-tuple-element.95.own_in.other_in, bf16[1024,768]{1,0:T(8,128)(2,1)} %get-tuple-element.95.own_in.other_in), custom_call_target="tpu_custom_call" | custom-call | flops 1207959552 | bytes 4325376 | tf_op jit(solution)/shard_map/grad_out/pallas_call | solution.py:474
  252.3 5.3 %collective-permute-done.26 = bf16[2,48,1152]{2,1,0:T(8,128)(2,1)S(1)} collective-permute-done((bf16[2,48,1152]{2,1,0:T(8,128)(2,1)}, bf16[2,48,1152]{2,1,0:T(8,128)(2,1)S(1)}, u32[]{:S(2)}, u32[]{:S(2)}) %collective-permute-start.26) | collective-permute-done | bytes 221216 | tf_op jit(solution)/shard_map/ppermute | solution.py:582
  270.3 9.7 %collective-permute-done.31 = bf16[2,48,1152]{2,1,0:T(8,128)(2,1)S(1)} collective-permute-done((bf16[2,48,1152]{2,1,0:T(8,128)(2,1)S(1)}, bf16[2,48,1152]{2,1,0:T(8,128)(2,1)S(1)}, u32[]{:S(2)}, u32[]{:S(2)}) %collective-permute-start.31) | collective-permute-done | bytes 221216 | tf_op jit(solution)/shard_map/ppermute | solution.py:582
  285.4 7.3 %add_fc1.1 = (bf16[2,48,1920]{2,1,0:T(8,128)(2,1)}, bf16[2,48,1920]{2,1,0:T(8,128)(2,1)}, bf16[2,48,1920]{2,1,0:T(8,128)(2,1)}, bf16[2,48,1920]{2,1,0:T(8,128)(2...) custom-call(bf16[16,48,1536]{2,1,0:T(8,128)(2,1)} %get-tuple-element, ...), custom_call_target="tpu_custom_call" | custom-call | flops 1474560 | bytes 8847360 | tf_op jit(solution)/shard_map/add_fc1/pallas_call | solution.py:564
  296.6 6.7 %add_fc2.1 = (bf16[2,48,1536]{2,1,0:T(8,128)(2,1)}, bf16[2,48,1536]{2,1,0:T(8,128)(2,1)}, bf16[2,48,1536]{2,1,0:T(8,128)(2,1)}, bf16[2,48,1536]{2,1,0:T(8,128)(2...) custom-call(bf16[16,48,1536]{2,1,0:T(8,128)(2,1)} %bitcast.103, ...), custom_call_target="tpu_custom_call" | custom-call | flops 1179648 | bytes 7077888 | tf_op jit(solution)/shard_map/add_fc2/pallas_call | solution.py:564
  305.8 10.4 %collective-permute-done.49 = bf16[2,48,1536]{2,1,0:T(8,128)(2,1)S(1)} collective-permute-done((bf16[2,48,1536]{2,1,0:T(8,128)(2,1)}, bf16[2,48,1536]{2,1,0:T(8,128)(2,1)S(1)}, u32[]{:S(2)}, u32[]{:S(2)}) %collective-permute-start.49) | collective-permute-done | bytes 294944 | tf_op jit(solution)/shard_map/ppermute | solution.py:582
  322.7 4.4 %collective-permute-done.40 = bf16[2,48,1920]{2,1,0:T(8,128)(2,1)S(1)} collective-permute-done((bf16[2,48,1920]{2,1,0:T(8,128)(2,1)}, bf16[2,48,1920]{2,1,0:T(8,128)(2,1)S(1)}, u32[]{:S(2)}, u32[]{:S(2)}) %collective-permute-start.40) | collective-permute-done | bytes 368672 | tf_op jit(solution)/shard_map/ppermute | solution.py:582
  327.1 7.1 %collective-permute-start.34 = (bf16[2,48,1152]{2,1,0:T(8,128)(2,1)S(1)}, bf16[2,48,1152]{2,1,0:T(8,128)(2,1)S(1)}, u32[]{:S(2)}, u32[]{:S(2)}) collective-permute-start(bf16[2,48,1152]{2,1,0:T(8,128)(2,1)S(1)} %pad_maximum_fusion.7), channel_id=1, source_target_pairs={{0,8},{8,0},{16,24},{24,16},{1,9},{9,1},{17,25},{25,17},{2,10},{10... | collective-permute-start | bytes 663560 | tf_op jit(solution)/shard_map/ppermute | solution.py:582
  337.8 5.7 %collective-permute-done.52 = bf16[2,48,1536]{2,1,0:T(8,128)(2,1)S(1)} collective-permute-done((bf16[2,48,1536]{2,1,0:T(8,128)(2,1)S(1)}, bf16[2,48,1536]{2,1,0:T(8,128)(2,1)S(1)}, u32[]{:S(2)}, u32[]{:S(2)}) %collective-permute-start.52) | collective-permute-done | bytes 294944 | tf_op jit(solution)/shard_map/ppermute | solution.py:582
  347.1 6.4 %collective-permute-done.41 = bf16[2,48,1920]{2,1,0:T(8,128)(2,1)S(1)} collective-permute-done((bf16[2,48,1920]{2,1,0:T(8,128)(2,1)S(1)}, bf16[2,48,1920]{2,1,0:T(8,128)(2,1)S(1)}, u32[]{:S(2)}, u32[]{:S(2)}) %collective-permute-start.41) | collective-permute-done | bytes 368672 | tf_op jit(solution)/shard_map/ppermute | solution.py:582
  355.5 11.4 %collective-permute-done.54 = bf16[2,48,1536]{2,1,0:T(8,128)(2,1)S(1)} collective-permute-done((bf16[2,48,1536]{2,1,0:T(8,128)(2,1)S(1)}, bf16[2,48,1536]{2,1,0:T(8,128)(2,1)S(1)}, u32[]{:S(2)}, u32[]{:S(2)}) %collective-permute-start.54) | collective-permute-done | bytes 294944 | tf_op jit(solution)/shard_map/ppermute | solution.py:582
  369.3 5.6 %collective-permute-done.43 = bf16[2,48,1920]{2,1,0:T(8,128)(2,1)S(1)} collective-permute-done((bf16[2,48,1920]{2,1,0:T(8,128)(2,1)S(1)}, bf16[2,48,1920]{2,1,0:T(8,128)(2,1)S(1)}, u32[]{:S(2)}, u32[]{:S(2)}) %collective-permute-start.43) | collective-permute-done | bytes 368672 | tf_op jit(solution)/shard_map/ppermute | solution.py:582
  393.3 13.8 %image_block.1 = bf16[256,768]{1,0:T(8,128)(2,1)} custom-call(s32[3]{0:T(128)} %pad_add_fusion.place, bf16[256,768]{1,0:T(8,128)(2,1)} %bitcast.115, f32[16,768]{1,0:T(8,128)} %convert_element_type.230.vec_ref, bf16[32,48,4608]{2,1,0:T(8,128)(2,1)} %bitcast.99), custom_call_target="tpu_custom_call" | custom-call | flops 3623878656 | bytes 14942208 | tf_op jit(solution)/shard_map/image_block/pallas_call | solution.py:770
  (300 shorter events, 126.9 us)
Async XLA Ops:
  7.3 107.2 %all-gather.5.cloned.1.call-start = ((), (), s32[]{:S(2)}) async-start(), calls=%async_computation | async-start | bytes 10948608 | tf_op jit(solution)/shard_map/all_gather | solution.py:736
  13.1 380.3 %all-gather.7.cloned.1.call-start = ((), (), s32[]{:S(2)}) async-start(), calls=%async_computation.1 | async-start | bytes 14598144 | tf_op jit(solution)/shard_map/all_gather | solution.py:738
  27.4 15.1 %collective-permute-start.4 = (bf16[2,48,1152]{2,1,0:T(8,128)(2,1)S(1)}, bf16[2,48,1152]{2,1,0:T(8,128)(2,1)S(1)}, u32[]{:S(2)}, u32[]{:S(2)}) collective-permute-start(bf16[2,48,1152]{2,1,0:T(8,128)(2,1)S(1)} %pad_maximum_fusion.6.rest_0_), channel_id=1, source_target_pairs={{0,4},{1,5},{2,6},{3,7},{4,0},{5,1},{6,2},{7,3},{8,12},{9,13},{10,... | collective-permute-start | bytes 663560 | tf_op jit(solution)/shard_map/ppermute | solution.py:582
  31.8 13.3 %collective-permute-start.7 = (bf16[2,48,1152]{2,1,0:T(8,128)(2,1)S(1)}, bf16[2,48,1152]{2,1,0:T(8,128)(2,1)S(1)}, u32[]{:S(2)}, u32[]{:S(2)}) collective-permute-start(bf16[2,48,1152]{2,1,0:T(8,128)(2,1)S(1)} %pad_maximum_fusion.6.rest_0_), channel_id=1, source_target_pairs={{0,16},{8,24},{16,0},{24,8},{1,17},{9,25},{17,1},{25,9},{2,18},{10... | collective-permute-start | bytes 663560 | tf_op jit(solution)/shard_map/ppermute | solution.py:582
  31.9 14.5 %collective-permute-start.11 = (bf16[2,48,1152]{2,1,0:T(8,128)(2,1)S(1)}, bf16[2,48,1152]{2,1,0:T(8,128)(2,1)S(1)}, u32[]{:S(2)}, u32[]{:S(2)}) collective-permute-start(bf16[2,48,1152]{2,1,0:T(8,128)(2,1)S(1)} %pad_maximum_fusion.6.rest_0_), channel_id=1, source_target_pairs={{0,8},{8,0},{16,24},{24,16},{1,9},{9,1},{17,25},{25,17},{2,10},{10... | collective-permute-start | bytes 663560 | tf_op jit(solution)/shard_map/ppermute | solution.py:582
  43.9 18.0 %collective-permute-start.12 = (bf16[2,48,1152]{2,1,0:T(8,128)(2,1)S(1)}, bf16[2,48,1152]{2,1,0:T(8,128)(2,1)S(1)}, u32[]{:S(2)}, u32[]{:S(2)}) collective-permute-start(bf16[2,48,1152]{2,1,0:T(8,128)(2,1)S(1)} %collective-permute-done.4.rest_1_), channel_id=1, source_target_pairs={{0,8},{8,0},{16,24},{24,16},{1,9},{9,1},{17,25},{25,17},{2,10},{10... | collective-permute-start | bytes 663560 | tf_op jit(solution)/shard_map/ppermute | solution.py:582
  46.4 15.7 %collective-permute-start.13 = (bf16[2,48,1152]{2,1,0:T(8,128)(2,1)S(1)}, bf16[2,48,1152]{2,1,0:T(8,128)(2,1)S(1)}, u32[]{:S(2)}, u32[]{:S(2)}) collective-permute-start(bf16[2,48,1152]{2,1,0:T(8,128)(2,1)S(1)} %collective-permute-done.5.rest_2_), channel_id=1, source_target_pairs={{0,8},{8,0},{16,24},{24,16},{1,9},{9,1},{17,25},{25,17},{2,10},{10... | collective-permute-start | bytes 663560 | tf_op jit(solution)/shard_map/ppermute | solution.py:582
  49.0 13.5 %collective-permute-start.10 = (bf16[2,48,1152]{2,1,0:T(8,128)(2,1)S(1)}, bf16[2,48,1152]{2,1,0:T(8,128)(2,1)S(1)}, u32[]{:S(2)}, u32[]{:S(2)}) collective-permute-start(bf16[2,48,1152]{2,1,0:T(8,128)(2,1)S(1)} %collective-permute-done.8.rest_5_), channel_id=1, source_target_pairs={{0,1},{1,0},{2,3},{3,2},{4,5},{5,4},{6,7},{7,6},{8,9},{9,8},{10,11... | collective-permute-start | bytes 663560 | tf_op jit(solution)/shard_map/ppermute | solution.py:582
  49.9 14.2 %collective-permute-start.15 = (bf16[2,48,1152]{2,1,0:T(8,128)(2,1)S(1)}, bf16[2,48,1152]{2,1,0:T(8,128)(2,1)S(1)}, u32[]{:S(2)}, u32[]{:S(2)}) collective-permute-start(bf16[2,48,1152]{2,1,0:T(8,128)(2,1)S(1)} %collective-permute-done.7.rest_4_), channel_id=1, source_target_pairs={{0,8},{8,0},{16,24},{24,16},{1,9},{9,1},{17,25},{25,17},{2,10},{10... | collective-permute-start | bytes 663560 | tf_op jit(solution)/shard_map/ppermute | solution.py:582
  200.3 23.7 %collective-permute-start.24 = (bf16[16,48,1152]{2,1,0:T(8,128)(2,1)}, bf16[16,48,1152]{2,1,0:T(8,128)(2,1)S(1)}, u32[]{:S(2)}, u32[]{:S(2)}) collective-permute-start(bf16[16,48,1152]{2,1,0:T(8,128)(2,1)} %get-tuple-element.82), channel_id=1, source_target_pairs={{0,8},{8,0},{16,24},{24,16},{1,9},{9,1},{17,25},{25,17},{2,10},{10... | collective-permute-start | bytes 5308424 | tf_op jit(solution)/shard_map/ppermute | solution.py:582
  220.0 24.5 %collective-permute-start.22 = (f32[12,96]{1,0:T(8,128)S(1)}, f32[12,96]{1,0:T(8,128)S(1)}, u32[]{:S(2)}, u32[]{:S(2)}) collective-permute-start(f32[12,96]{1,0:T(8,128)S(1)} %add_bitcast_fusion), channel_id=1, source_target_pairs={{0,8},{8,0},{16,24},{24,16},{1,9},{9,1},{17,25},{25,17},{2,10},{10... | collective-permute-start | bytes 13832 | tf_op jit(solution)/shard_map/ppermute | solution.py:582
  231.5 20.3 %collective-permute-start.28 = (bf16[2,48,1152]{2,1,0:T(8,128)(2,1)}, bf16[2,48,1152]{2,1,0:T(8,128)(2,1)S(1)}, u32[]{:S(2)}, u32[]{:S(2)}) collective-permute-start(bf16[2,48,1152]{2,1,0:T(8,128)(2,1)} %get-tuple-element.89), channel_id=1, source_target_pairs={{0,1},{1,0},{2,3},{3,2},{4,5},{5,4},{6,7},{7,6},{8,9},{9,8},{10,11... | collective-permute-start | bytes 663560 | tf_op jit(solution)/shard_map/ppermute | solution.py:582
  244.1 40.4 %collective-permute-start.35 = (bf16[16,48,1536]{2,1,0:T(8,128)(2,1)}, bf16[16,48,1536]{2,1,0:T(8,128)(2,1)}, u32[]{:S(2)}, u32[]{:S(2)}) collective-permute-start(bf16[16,48,1536]{2,1,0:T(8,128)(2,1)} %get-tuple-element.94), channel_id=1, source_target_pairs={{0,8},{8,0},{16,24},{24,16},{1,9},{9,1},{17,25},{25,17},{2,10},{10... | collective-permute-start | bytes 7077896 | tf_op jit(solution)/shard_map/ppermute | solution.py:582
  250.2 34.3 %collective-permute-start.36 = (bf16[16,48,384]{2,1,0:T(8,128)(2,1)}, bf16[16,48,384]{2,1,0:T(8,128)(2,1)S(1)}, u32[]{:S(2)}, u32[]{:S(2)}) collective-permute-start(bf16[16,48,384]{2,1,0:T(8,128)(2,1)} %get-tuple-element.97), channel_id=1, source_target_pairs={{0,8},{8,0},{16,24},{24,16},{1,9},{9,1},{17,25},{25,17},{2,10},{10... | collective-permute-start | bytes 1769480 | tf_op jit(solution)/shard_map/ppermute | solution.py:582
  250.7 44.5 %collective-permute-start.47 = (bf16[16,48,1536]{2,1,0:T(8,128)(2,1)}, bf16[16,48,1536]{2,1,0:T(8,128)(2,1)S(1)}, u32[]{:S(2)}, u32[]{:S(2)}) collective-permute-start(bf16[16,48,1536]{2,1,0:T(8,128)(2,1)} %bitcast.139), channel_id=1, source_target_pairs={{0,8},{8,0},{16,24},{24,16},{1,9},{9,1},{17,25},{25,17},{2,10},{10... | collective-permute-start | bytes 7077896 | tf_op jit(solution)/shard_map/ppermute | solution.py:582
  281.4 22.4 %collective-permute-start.32 = (bf16[48,1152]{1,0:T(8,128)(2,1)}, bf16[48,1152]{1,0:T(8,128)(2,1)}, u32[]{:S(2)}, u32[]{:S(2)}) collective-permute-start(bf16[48,1152]{1,0:T(8,128)(2,1)} %fusion.15), channel_id=1, source_target_pairs={{0,2},{1,3},{2,0},{3,1},{4,6},{5,7},{6,4},{7,5},{8,10},{9,11},{10,... | collective-permute-start | bytes 331784 | tf_op jit(solution)/shard_map/ppermute | solution.py:582
  292.7 28.8 %collective-permute-start.38 = (bf16[2,48,1920]{2,1,0:T(8,128)(2,1)}, bf16[2,48,1920]{2,1,0:T(8,128)(2,1)S(1)}, u32[]{:S(2)}, u32[]{:S(2)}) collective-permute-start(bf16[2,48,1920]{2,1,0:T(8,128)(2,1)} %get-tuple-element.101), channel_id=1, source_target_pairs={{0,16},{8,24},{16,0},{24,8},{1,17},{9,25},{17,1},{25,9},{2,18},{10... | collective-permute-start | bytes 1105928 | tf_op jit(solution)/shard_map/ppermute | solution.py:582
  293.7 61.7 %collective-permute-start.37 = (bf16[2,48,1920]{2,1,0:T(8,128)(2,1)}, bf16[2,48,1920]{2,1,0:T(8,128)(2,1)S(1)}, u32[]{:S(2)}, u32[]{:S(2)}) collective-permute-start(bf16[2,48,1920]{2,1,0:T(8,128)(2,1)} %get-tuple-element.99), channel_id=1, source_target_pairs={{0,16},{8,24},{16,0},{24,8},{1,17},{9,25},{17,1},{25,9},{2,18},{10... | collective-permute-start | bytes 1105928 | tf_op jit(solution)/shard_map/ppermute | solution.py:582
  294.1 53.0 %collective-permute-start.42 = (bf16[2,48,1920]{2,1,0:T(8,128)(2,1)}, bf16[2,48,1920]{2,1,0:T(8,128)(2,1)S(1)}, u32[]{:S(2)}, u32[]{:S(2)}) collective-permute-start(bf16[2,48,1920]{2,1,0:T(8,128)(2,1)} %get-tuple-element.105), channel_id=1, source_target_pairs={{0,1},{1,0},{2,3},{3,2},{4,5},{5,4},{6,7},{7,6},{8,9},{9,8},{10,11... | collective-permute-start | bytes 1105928 | tf_op jit(solution)/shard_map/ppermute | solution.py:582
  303.7 17.2 %collective-permute-start.51 = (bf16[2,48,1536]{2,1,0:T(8,128)(2,1)}, bf16[2,48,1536]{2,1,0:T(8,128)(2,1)S(1)}, u32[]{:S(2)}, u32[]{:S(2)}) collective-permute-start(bf16[2,48,1536]{2,1,0:T(8,128)(2,1)} %get-tuple-element.114), channel_id=1, source_target_pairs={{0,1},{1,0},{2,3},{3,2},{4,5},{5,4},{6,7},{7,6},{8,9},{9,8},{10,11... | collective-permute-start | bytes 884744 | tf_op jit(solution)/shard_map/ppermute | solution.py:582
  321.0 23.8 %collective-permute-start.48 = (bf16[2,48,1536]{2,1,0:T(8,128)(2,1)S(1)}, bf16[2,48,1536]{2,1,0:T(8,128)(2,1)S(1)}, u32[]{:S(2)}, u32[]{:S(2)}) collective-permute-start(bf16[2,48,1536]{2,1,0:T(8,128)(2,1)S(1)} %copy-done.33), channel_id=1, source_target_pairs={{0,16},{8,24},{16,0},{24,8},{1,17},{9,25},{17,1},{25,9},{2,18},{10... | collective-permute-start | bytes 884744 | tf_op jit(solution)/shard_map/ppermute | solution.py:582
  321.5 16.0 %collective-permute-start.53 = (bf16[2,48,1536]{2,1,0:T(8,128)(2,1)S(1)}, bf16[2,48,1536]{2,1,0:T(8,128)(2,1)S(1)}, u32[]{:S(2)}, u32[]{:S(2)}) collective-permute-start(bf16[2,48,1536]{2,1,0:T(8,128)(2,1)S(1)} %copy-done.34), channel_id=1, source_target_pairs={{0,1},{1,0},{2,3},{3,2},{4,5},{5,4},{6,7},{7,6},{8,9},{9,8},{10,11... | collective-permute-start | bytes 884744 | tf_op jit(solution)/shard_map/ppermute | solution.py:582
  345.3 21.6 %collective-permute-start.54 = (bf16[2,48,1536]{2,1,0:T(8,128)(2,1)S(1)}, bf16[2,48,1536]{2,1,0:T(8,128)(2,1)S(1)}, u32[]{:S(2)}, u32[]{:S(2)}) collective-permute-start(bf16[2,48,1536]{2,1,0:T(8,128)(2,1)S(1)} %add_convert_fusion.3), channel_id=1, source_target_pairs={{0,4},{1,5},{2,6},{3,7},{4,0},{5,1},{6,2},{7,3},{8,12},{9,13},{10,... | collective-permute-start | bytes 884744 | tf_op jit(solution)/shard_map/ppermute | solution.py:582
  353.6 21.2 %collective-permute-start.43 = (bf16[2,48,1920]{2,1,0:T(8,128)(2,1)S(1)}, bf16[2,48,1920]{2,1,0:T(8,128)(2,1)S(1)}, u32[]{:S(2)}, u32[]{:S(2)}) collective-permute-start(bf16[2,48,1920]{2,1,0:T(8,128)(2,1)S(1)} %add_convert_fusion), channel_id=1, source_target_pairs={{0,4},{1,5},{2,6},{3,7},{4,0},{5,1},{6,2},{7,3},{8,12},{9,13},{10,... | collective-permute-start | bytes 1105928 | tf_op jit(solution)/shard_map/ppermute | solution.py:582
  (84 other events, 830.4 us)
Sparse Core Ops, SparseCore 0:
  13.2 101.3 all-gather.4
  117.4 101.9 all-gather.6
